TPU v7x, 32 devices: a whole 2x2x4 slice. The times are simulated.
32 devices in a mesh: groups: 2 (over y), expert: 4 (over z), rep: 4 (over x, core).
Axes of the slice: x: 2, y: 2, z: 4, core: 2. Of those that a mesh axis runs over, the one named last changes fastest.
Arguments:
- tokens: bfloat16 [128, 4096], P(('groups', 'expert', 'rep')), parts along dimension 0, may hold values from -6 to 6
- expert_ids: int32 [128, 8], P(('groups', 'expert', 'rep')), parts along dimension 0, may hold values from 0 to 31, as said below
- route_probs: float32 [128, 8], P(('groups', 'expert', 'rep')), parts along dimension 0, may hold values from 0.3 to 1
- gate_weight: bfloat16 [32, 1536, 4096], P('expert', 'rep'), may hold values from -0.09375 to 0.09375
- up_weight: bfloat16 [32, 1536, 4096], P('expert', 'rep'), may hold values from -0.09375 to 0.09375
- down_weight: bfloat16 [32, 1536, 4096], P('expert', 'rep'), may hold values from -0.15625 to 0.15625
Outputs:
- moe_out: bfloat16 [128, 4096], P(('groups', 'expert', 'rep')), parts along dimension 0
There are 2 independent parts, one for each index of `groups`. A program takes and returns all parts, laid end to end along the dimension named above; an argument that names none is the same for every part. Nothing has to cross between parts.
Inputs may be any that keep to these rules, and one draw needn't show every extreme that they name: `expert_ids`: each row names 8 different experts. Among the rows of one device no expert is named more than 3 times, and some expert is named exactly 3 times among the rows of every device.
All inputs are finite; a program needn't handle non-finite values.
Results may differ from a plain program's by a relative error of at most 0.0058.
Values may be sent and summed in bfloat16 or wider, within the bound.
No kernel may reach another device: no remote copies, remote signals or barrier semaphores. Data moves between devices by JAX's collectives and lax.ppermute only.
A program may use at most 128 MiB of HBM per device.

v0:
```python
import jax
import jax.numpy as jnp
from jax import lax
from jax.sharding import PartitionSpec as P

CAP = 3


def slot_numbers(route_ids, experts):
    flat_ids = route_ids.reshape(-1)
    one_hot = (flat_ids[:, None] == jnp.arange(experts, dtype=jnp.int32)[None, :]).astype(jnp.int32)
    running = jnp.cumsum(one_hot, axis=0)
    return (jnp.sum(running * one_hot, axis=1) - 1).reshape(route_ids.shape)


def dispatch_matrix(slot_place, slot_count):
    top_count = slot_place.shape[1]
    targets = jnp.arange(slot_count, dtype=jnp.int32)[:, None] == slot_place.reshape(-1)[None, :]
    return jnp.any(targets.reshape(slot_count, slot_place.shape[0], top_count), axis=2).astype(
        jnp.bfloat16
    )


def expert_block(block_rows, gate_weight, up_weight, down_weight):
    gate_proj = jnp.einsum(
        "sjncd,jhd->sjnch", block_rows, gate_weight, preferred_element_type=jnp.float32
    )
    up_proj = jnp.einsum(
        "sjncd,jhd->sjnch", block_rows, up_weight, preferred_element_type=jnp.float32
    )
    hidden = (jax.nn.silu(gate_proj) * up_proj).astype(jnp.bfloat16)
    return jnp.einsum(
        "sjnch,jhd->sjncd", hidden, down_weight, preferred_element_type=jnp.float32
    ).astype(jnp.bfloat16)


def combine_rows(source_rows, slot_place, weights):
    running_sum = jnp.zeros((slot_place.shape[0], source_rows.shape[1]), jnp.float32)
    for column in range(slot_place.shape[1]):
        running_sum = running_sum + weights[:, column : column + 1] * jnp.take(
            source_rows, slot_place[:, column], axis=0
        )
    return running_sum


def local(tokens, expert_ids, route_probs, gate_weight, up_weight, down_weight):
    model_width = tokens.shape[1]
    local_experts = gate_weight.shape[0]
    expert_devices = lax.axis_size("expert")
    experts = local_experts * expert_devices
    capacity = CAP
    own_slots = slot_numbers(expert_ids, experts)
    own_place = expert_ids * capacity + own_slots
    dispatch_table = dispatch_matrix(own_place, experts * capacity)
    outgoing = jnp.dot(dispatch_table, tokens, preferred_element_type=jnp.float32).astype(
        jnp.bfloat16
    )
    outgoing = outgoing.reshape(expert_devices, local_experts, 1, capacity, model_width)
    arrived = lax.all_to_all(outgoing, "expert", split_axis=0, concat_axis=0, tiled=True)
    partials = expert_block(
        lax.all_gather(arrived, "rep", axis=2, tiled=True), gate_weight, up_weight, down_weight
    )
    swapped = lax.all_to_all(partials, "rep", split_axis=2, concat_axis=2, tiled=True)
    summed = jnp.sum(swapped, axis=2, dtype=jnp.float32)
    returned = lax.all_to_all(summed, "expert", split_axis=0, concat_axis=0, tiled=True)
    own_index = expert_ids * capacity + own_slots
    weights = route_probs / jnp.sum(route_probs, axis=1, keepdims=True)
    combined = combine_rows(returned.reshape(experts * capacity, model_width), own_index, weights)
    return combined.astype(jnp.bfloat16)


def solution(mesh):
    return jax.shard_map(
        local,
        mesh=mesh,
        in_specs=(
            P(("groups", "expert", "rep"), None),
            P(("groups", "expert", "rep"), None),
            P(("groups", "expert", "rep"), None),
            P("expert", "rep", None),
            P("expert", "rep", None),
            P("expert", "rep", None),
        ),
        out_specs=P(("groups", "expert", "rep"), None),
        check_vma=False,
    )
```

profile of v0, /device:TPU:0, one launch (start us, length us, event | category | flops | bytes accessed | tf_op | source)
XLA Modules:
  0.0 213.6 jit_solution(7310337685762500697)
XLA Ops:
  6.5 0.0 copy-start
  6.5 0.0 all-gather.2.cloned.1.call-start
  6.5 0.8 eq.30
  7.3 0.1 fusion.42
  7.4 0.1 reduce_window_sum.11
  7.4 0.2 select_reduce_fusion
  7.6 0.1 sub.7
  7.7 0.7 multiply_add_fusion
  8.4 0.1 fusion.43
  8.5 0.0 copy-done
  8.5 0.4 convolution_convert_fusion
  8.9 0.5 reshape.27
  9.4 0.6 copy.25
  10.0 26.3 %all_to_all.15 = bf16[4,8,1,3,4096]{4,1,3,2,0:T(8,128)(2,1)} all-to-all(bf16[4,8,1,3,4096]{4,1,3,2,0:T(8,128)(2,1)S(1)} %copy.25), channel_id=1, replica_groups=mesh['groups'=2,'expert'=4,'rep'=4] {'expert'}, dimensions={0} | all-to-all | bytes 1572864 | tf_op jit(solution)/shard_map/all_to_all | solution.py:59
  36.4 0.0 all-gather.2.cloned.1.call-update
  36.4 27.8 %all-gather.2.cloned.1.call-done = bf16[4,8,4,3,4096]{4,1,3,0,2:T(8,128)(2,1)} async-done(((bf16[4,8,1,3,4096]{4,1,3,0,2:T(8,128)(2,1)}), bf16[4,8,4,3,4096]{4,1,3,0,2:T(8,128)(2,1)}) %all-gather.2.cloned.1.call-update) | async-done | bytes 3145744 | tf_op jit(solution)/shard_map/all_gather | solution.py:61
  64.2 16.3 %fusion.14 = f32[4,8,4,3,384]{4,2,3,0,1:T(4,128)S(1)} fusion(bf16[8,384,4096]{2,1,0:T(8,128)(2,1)} %param.11, bf16[4,8,4,3,4096]{4,1,3,0,2:T(8,128)(2,1)} %all-gather.2.cloned.1.call-done), kind=kOutput, calls=%fused_computation.20 | convolution fusion | flops 1207959552 | bytes 28901376 | tf_op jit(solution)/shard_map/sjncd,jhd->sjnch/dot_general | solution.py:25
  80.5 16.7 %fusion.29 = bf16[4,8,4,3,384]{4,2,3,0,1:T(4,128)(2,1)S(1)} fusion(bf16[8,384,4096]{2,1,0:T(8,128)(2,1)} %param.12, bf16[4,8,4,3,4096]{4,1,3,0,2:T(8,128)(2,1)} %all-gather.2.cloned.1.call-done, f32[4,8,4,3,384]{4,2,3,0,1:T(4,128)S(1)} %fusion.14), kind=kOutput, calls=%fused_computation.23 | convolution fusion | flops 1208844288 | bytes 29196288 | tf_op jit(solution)/shard_map/sjncd,jhd->sjnch/dot_general | solution.py:28
  97.2 12.5 %fusion.9 = bf16[4,8,4,3,4096]{4,2,3,0,1:T(4,128)(2,1)S(1)} fusion(bf16[4,8,4,3,384]{4,2,3,0,1:T(4,128)(2,1)S(1)} %fusion.29, bf16[8,384,4096]{2,1,0:T(8,128)(2,1)} %param.13), kind=kOutput, calls=%fused_computation.16 | convolution fusion | flops 1209532416 | bytes 28606464 | tf_op jit(solution)/shard_map/sjnch,jhd->sjncd/dot_general | solution.py:32
  109.7 3.4 %copy.29 = bf16[4,8,4,3,4096]{4,1,3,0,2:T(8,128)(2,1)} copy(bf16[4,8,4,3,4096]{4,2,3,0,1:T(4,128)(2,1)S(1)} %fusion.9) | data formatting | bytes 6291456 | tf_op jit(solution)/shard_map/convert_element_type | solution.py:34
  113.1 3.7 %all-to-all-start.1 = ((bf16[4,8,4,3,4096]{4,1,3,0,2:T(8,128)(2,1)}), bf16[4,8,4,3,4096]{4,1,3,0,2:T(8,128)(2,1)S(1)}, u32[]{:S(2)}, u32[]{:S(2)}) async-start(bf16[4,8,4,3,4096]{4,1,3,0,2:T(8,128)(2,1)} %copy.29), calls=%async_computation.1 | async-start | bytes 6291456 | tf_op jit(solution)/shard_map/all_to_all | solution.py:63
  116.8 0.3 slice_reduce_fusion.14
  117.1 0.0 copy-start.2
  117.1 36.6 %all-to-all-done.1 = bf16[4,8,4,3,4096]{4,1,3,0,2:T(8,128)(2,1)S(1)} async-done(((bf16[4,8,4,3,4096]{4,1,3,0,2:T(8,128)(2,1)}), bf16[4,8,4,3,4096]{4,1,3,0,2:T(8,128)(2,1)S(1)}, u32[]{:S(2)}, u32[]{:S(2)}) %all-to-all-start.1) | async-done | bytes 3145760 | tf_op jit(solution)/shard_map/all_to_all | solution.py:63
  153.7 1.7 convert_reduce_fusion
  155.4 4.6 %all-to-all-start.2 = ((f32[4,8,3,4096]{3,1,2,0:T(8,128)}), f32[4,8,3,4096]{3,1,2,0:T(8,128)S(1)}, u32[]{:S(2)}, u32[]{:S(2)}) async-start(f32[4,8,3,4096]{3,1,2,0:T(8,128)} %convert_reduce_fusion), calls=%async_computation.2 | async-start | bytes 3145728 | tf_op jit(solution)/shard_map/all_to_all | solution.py:65
  160.0 0.0 copy-done.2
  160.0 0.1 reduce_sum.27
  160.2 0.1 broadcast_divide_fusion
  160.3 0.3 slice_reduce_fusion.15
  160.6 36.1 %all-to-all-done.2 = f32[4,8,3,4096]{3,1,2,0:T(8,128)S(1)} async-done(((f32[4,8,3,4096]{3,1,2,0:T(8,128)}), f32[4,8,3,4096]{3,1,2,0:T(8,128)S(1)}, u32[]{:S(2)}, u32[]{:S(2)}) %all-to-all-start.2) | async-done | bytes 1572896 | tf_op jit(solution)/shard_map/all_to_all | solution.py:65
  196.7 2.4 %copy.32 = f32[4,8,3,4096]{3,2,1,0:T(4,128)} copy(f32[4,8,3,4096]{3,1,2,0:T(8,128)S(1)} %all-to-all-done.2) | data formatting | bytes 3145728 | tf_op jit(solution)/shard_map/all_to_all | solution.py:65
  199.2 0.0 copy-start.1
  199.2 2.0 reshape.28
  201.2 0.6 gather_fusion.7
  201.8 0.6 gather_fusion.6
  202.4 0.6 gather_fusion.5
  203.0 0.6 gather_fusion.4
  203.6 0.6 gather_fusion.3
  204.2 0.6 gather_fusion.2
  204.7 0.6 gather_fusion.1
  205.3 0.6 gather_fusion
  205.9 0.8 fusion.35
  206.7 0.0 copy-done.1
  (17 shorter events, 0.1 us)
Async XLA Ops:
  6.5 2.0 copy-start
  6.5 57.7 %all-gather.2.cloned.1.call-start = ((), (), s32[]{:S(2)}) async-start(), calls=%async_computation.3 | async-start | bytes 3932160 | tf_op jit(solution)/shard_map/all_gather | solution.py:61
  113.1 40.6 %all-to-all-start.1 = ((bf16[4,8,4,3,4096]{4,1,3,0,2:T(8,128)(2,1)}), bf16[4,8,4,3,4096]{4,1,3,0,2:T(8,128)(2,1)S(1)}, u32[]{:S(2)}, u32[]{:S(2)}) async-start(bf16[4,8,4,3,4096]{4,1,3,0,2:T(8,128)(2,1)} %copy.29), calls=%async_computation.1 | async-start | bytes 6291456 | tf_op jit(solution)/shard_map/all_to_all | solution.py:63
  117.1 42.8 %copy-start.2 = (f32[4,8]{1,0:T(4,128)S(1)}, f32[4,8]{1,0:T(4,128)}, u32[]{:S(2)}) copy-start(f32[4,8]{1,0:T(4,128)} %param.10) | copy-start | bytes 388
  155.4 41.4 %all-to-all-start.2 = ((f32[4,8,3,4096]{3,1,2,0:T(8,128)}), f32[4,8,3,4096]{3,1,2,0:T(8,128)S(1)}, u32[]{:S(2)}, u32[]{:S(2)}) async-start(f32[4,8,3,4096]{3,1,2,0:T(8,128)} %convert_reduce_fusion), calls=%async_computation.2 | async-start | bytes 3145728 | tf_op jit(solution)/shard_map/all_to_all | solution.py:65
  199.2 7.6 %copy-start.1 = (bf16[4,4096]{1,0:T(4,128)(2,1)S(1)}, bf16[4,4096]{1,0:T(4,128)(2,1)}, u32[]{:S(2)}) copy-start(bf16[4,4096]{1,0:T(4,128)(2,1)} %param.8) | copy-start | bytes 98308
Sparse Core Ops, SparseCore 0:
  36.5 27.6 all-gather.1
where the time goes:
time: 214 us
  waiting for transfers between devices  100 us (47%)
  matrix products  45.9 us (21%)
  blocking collectives  26.3 us (12%)
  local copies, waits for them, and re-layouts  15.1 us (7%)
  between operations  13.6 us (6%)
  starting transfers between devices  8.29 us (4%)
  other arithmetic  3.86 us (2%)
    all_to_all x1, waiting for transfers between devices, local(): lax.all_to_all(partials, 'rep', split_axis=2, concat_axis=2, tiled=True)  36.6 us
    all_to_all x1, waiting for transfers between devices, local(): lax.all_to_all(summed, 'expert', split_axis=0, concat_axis=0, tiled=True)  36.1 us
    all_gather x1, waiting for transfers between devices, local(): lax.all_gather(arrived, 'rep', axis=2, tiled=True)  27.8 us
    all_to_all x1, blocking collectives, local(): lax.all_to_all(outgoing, 'expert', split_axis=0, concat_axis=0, tiled=True)  26.3 us
    dot_general x1, matrix products, expert_block(): jnp.einsum('sjncd,jhd->sjnch', block_rows, up_weight, preferred_element_t...  16.7 us
    dot_general x1, matrix products, expert_block(): jnp.einsum('sjncd,jhd->sjnch', block_rows, gate_weight, preferred_element...  16.3 us
    dot_general x1, matrix products, expert_block(): jnp.einsum('sjnch,jhd->sjncd', hidden, down_weight, preferred_element_typ...  12.5 us
    gather x8, local copies, waits for them, and re-layouts, combine_rows(): jnp.take(source_rows, slot_place[:, column], axis=0)  4.68 us
  transfers between devices with their start and end apart: 3, of which 3 were waited for; matrix products, arithmetic and copies ran while one was open for 0% of the time, Pallas kernels for 0%

commit v1 on v0

v1 whole, which is shorter than its diff:
```python
import functools

import jax
import jax.numpy as jnp
from jax import lax
from jax.experimental import pallas as pl
from jax.experimental.pallas import tpu as pltpu
from jax.sharding import PartitionSpec as P

LANES = 128
PACK = 16
ROW_TILE = 128
VMEM_BYTES = 64 * 2**20
EARLY_CHUNKS = 5
RING_CHUNKS = 10
NT = (((1,), (1,)), ((), ()))
LINKED = ("expert", "rep")
VMEM = pl.BlockSpec(memory_space=pltpu.VMEM)
HBM = pl.BlockSpec(memory_space=pltpu.HBM)


def chip_pairs(chips):
    return [(k + 1, k) if k + 2 == chips else (k, k + 1) for k in range(chips - 2, 0, -2)], 1


def chip_perm(chips, first, second):
    return [
        (chip * 2 + core, ((chip ^ (second if core else first)) << 1) | core)
        for chip in range(chips)
        for core in (0, 1)
    ]


def core_perm(chips):
    return [(device, device ^ 1) for device in range(2 * chips)]


def in_vmem(array):
    return pltpu.with_memory_space_constraint(array, pltpu.VMEM)


def padded_lanes(experts):
    return -(-2 * experts // LANES) * LANES


def rows_kernel(experts, tokens_in, ids_in, probs_in, rows_ref, tokens_ref, ids_ref, probs_ref, sem):
    width = tokens_ref.shape[1]
    copies = [
        pltpu.make_async_copy(source, target, sem.at[index])
        for index, (source, target) in enumerate(
            [(ids_in, ids_ref), (probs_in, probs_ref), (tokens_in, tokens_ref)]
        )
    ]
    for copy in copies:
        copy.start()
    for copy in copies:
        copy.wait()
    probs = probs_ref[...]
    weights = probs / jnp.sum(probs, axis=1, keepdims=True)
    shape = (rows_ref.shape[0], rows_ref.shape[1] - width)
    lane = lax.broadcasted_iota(jnp.int32, shape, 1)
    expert = jnp.where(lane < experts, lane, lane - experts)
    dense = jnp.zeros(shape, jnp.float32)
    for column in range(probs.shape[1]):
        chosen = ids_ref[:, column : column + 1] == expert
        dense = dense + jnp.where(chosen, weights[:, column : column + 1], 0.0)
    high = dense.astype(jnp.bfloat16).astype(jnp.float32)
    rows_ref[:, :width] = tokens_ref[...]
    rows_ref[:, width:] = jnp.where(lane < experts, high, dense - high).astype(jnp.bfloat16)


def chunk_of(refs, local_experts, per_block, index):
    gate_ref, up_ref, down_ref = refs
    block, place = divmod(index, 3 * per_block)
    if place < 2 * per_block:
        return (gate_ref, up_ref)[place % 2].at[block * per_block + place // 2]
    return down_ref.at[block * per_block + place - 2 * per_block]


def early_kernel(per_block, after_ref, gate_ref, up_ref, down_ref, early_ref, sem):
    copies = [
        pltpu.make_async_copy(
            chunk_of((gate_ref, up_ref, down_ref), gate_ref.shape[0], per_block, index), early_ref.at[index], sem.at[index]
        )
        for index in range(early_ref.shape[0])
    ]
    for copy in copies:
        copy.start()
    for copy in copies:
        copy.wait()


def expert_kernel(pieces, per_block, experts, parts, *refs):
    row_refs = refs[:pieces]
    early_ref, gate_ref, up_ref, down_ref, own_ref, kept_ref, sent_ref, rows, total, ring, ring_sem = refs[pieces:]
    local_experts, expert_hidden, width = gate_ref.shape
    tokens = rows.shape[0]
    early, slots, chunks = early_ref.shape[0], ring.shape[0], 3 * local_experts

    def fetch(index):
        slot = (index - early) % slots
        return pltpu.make_async_copy(
            chunk_of((gate_ref, up_ref, down_ref), local_experts, per_block, index), ring.at[slot], ring_sem.at[slot]
        )

    def chunk(index):
        if index < early:
            return early_ref.at[index]
        fetch(index).wait()
        return ring.at[(index - early) % slots]

    def used(index):
        if index >= early and index + slots < chunks:
            fetch(index + slots).start()

    for index in range(early, min(early + slots, chunks)):
        fetch(index).start()

    route = []
    held, start = [], 0
    for ref in row_refs:
        held.append(ref[...].astype(jnp.float32))
        count = sum(piece.shape[0] for piece in held)
        if count % PACK == 0:
            joined = jnp.concatenate(held, axis=0) if len(held) > 1 else held[0]
            rows[start : start + count, :] = joined[:, :width].astype(jnp.bfloat16)
            route.append(joined[:, width:])
            held, start = [], start + count
    route = jnp.concatenate(route, axis=0).astype(jnp.bfloat16)
    lane = lax.broadcasted_iota(jnp.int32, (local_experts, route.shape[1]), 1)
    wanted = lax.axis_index("expert") * local_experts + lax.broadcasted_iota(
        jnp.int32, (local_experts, route.shape[1]), 0
    )
    chooser = ((lane == wanted) | (lane == wanted + experts)).astype(jnp.bfloat16)
    weights = lax.dot_general(chooser, route, NT, preferred_element_type=jnp.float32)

    part = width // parts
    half = expert_hidden // 2
    for block in range(local_experts // per_block):
        first = block * 3 * per_block
        hidden = []
        for index in range(per_block):
            expert = block * per_block + index
            gate_at, up_at = first + 2 * index, first + 2 * index + 1
            weight_refs = [chunk(gate_at), chunk(up_at)]
            gate, up = [
                [
                    lax.dot_general(
                        ref[start : start + half, :], rows[...], NT, preferred_element_type=jnp.float32
                    )
                    for start in (0, half)
                ]
                for ref in weight_refs
            ]
            used(gate_at)
            used(up_at)
            for g, u in zip(gate, up):
                hidden.append(g / (1.0 + jnp.exp(-g)) * u * weights[expert : expert + 1, :])
        hidden = jnp.concatenate(hidden, axis=0).T.astype(jnp.bfloat16)
        if tokens < ROW_TILE:
            hidden = jnp.concatenate([hidden, jnp.zeros((ROW_TILE - tokens, hidden.shape[1]), jnp.bfloat16)], axis=0)
        downs = [chunk(first + 2 * per_block + index) for index in range(per_block)]
        for index in range(parts):
            columns = pl.ds(index * part, part)
            down = [ref[:, columns] for ref in downs]
            down = jnp.concatenate(down, axis=0) if per_block > 1 else down[0]
            product = jnp.dot(hidden, down, preferred_element_type=jnp.float32)[:tokens]
            if block:
                total[:, columns] += product
            else:
                total[:, columns] = product
        for index in range(per_block):
            used(first + 2 * per_block + index)

    chip = own_ref.shape[0]
    exclusive = kept_ref.shape[0] - chip
    own_ref[...] = total[:chip, :]
    kept_ref[:exclusive, :] = total[chip : chip + exclusive, :]
    kept_ref[exclusive:, :] = total[tokens - chip :, :]
    sent_ref[...] = jnp.concatenate(
        [total[chip + exclusive : tokens - chip, :], total[tokens - chip :, :]], axis=0
    ).astype(jnp.bfloat16)


def chip_sum_kernel(kept_ref, arrived_ref, *out_refs):
    summed = kept_ref[...] + arrived_ref[...].astype(jnp.float32)
    chip_rows = out_refs[0].shape[0]
    for index, out_ref in enumerate(out_refs[:-1]):
        out_ref[...] = summed[index * chip_rows : (index + 1) * chip_rows, :].astype(jnp.bfloat16)
    half = out_refs[-1].shape[0]
    rows = kept_ref.shape[0]
    arrived = arrived_ref[...].astype(jnp.float32)
    out_refs[-1][...] = (
        kept_ref[rows - 2 * half : rows - half, :] + arrived[rows - half :, :]
    ).astype(jnp.bfloat16)


def token_sum_kernel(own_ref, shared_ref, *refs):
    piece_refs, mine_ref, other_ref = refs[:-2], refs[-2], refs[-1]
    total = own_ref[...]
    for ref in piece_refs:
        total = total + ref[...].astype(jnp.float32)
    half = mine_ref.shape[0]
    mine_ref[...] = total[:half, :] + shared_ref[...].astype(jnp.float32)
    other_ref[...] = total[half:, :]


def last_kernel(mine_ref, other_ref, out_ref):
    out_ref[...] = (mine_ref[...] + other_ref[...]).astype(jnp.bfloat16)


def call(kernel, out_shapes, *args, name):
    held = sum(array.size * 4 for array in [*args, *jax.tree.leaves(out_shapes)])
    return pl.pallas_call(
        kernel,
        out_shape=out_shapes,
        in_specs=[VMEM] * len(args),
        out_specs=jax.tree.map(lambda _: VMEM, out_shapes),
        compiler_params=pltpu.CompilerParams(vmem_limit_bytes=2 * held + 2**20),
        name=name,
    )(*args)


def local(tokens, expert_ids, route_probs, gate_weight, up_weight, down_weight):
    own_rows, width = tokens.shape
    local_experts, expert_hidden, _ = gate_weight.shape
    experts = local_experts * lax.axis_size("expert")
    chips = lax.axis_size("expert") * lax.axis_size("rep") // 2
    pairs, shared = chip_pairs(chips)
    swap = core_perm(chips)
    all_rows = 2 * own_rows * chips
    chip_rows = 2 * own_rows
    reduced = chip_rows * (len(pairs) + 1)
    per_block = 2 if local_experts % 2 == 0 else 1
    chunk_bytes = expert_hidden * width * 2
    chunks = 3 * local_experts
    early = min(EARLY_CHUNKS, chunks - 1)
    parts = max(2, all_rows // 64)

    mine = pl.pallas_call(
        functools.partial(rows_kernel, experts),
        out_shape=jax.ShapeDtypeStruct((own_rows, width + padded_lanes(experts)), jnp.bfloat16),
        in_specs=[pl.BlockSpec(memory_space=pl.ANY)] * 3,
        out_specs=VMEM,
        scratch_shapes=[pltpu.VMEM(array.shape, array.dtype) for array in (tokens, expert_ids, route_probs)]
        + [pltpu.SemaphoreType.DMA((3,))],
        compiler_params=pltpu.CompilerParams(vmem_limit_bytes=VMEM_BYTES - 2**16),
        name="rows",
    )(tokens, expert_ids, route_probs)
    shared_rows = lax.ppermute(mine, LINKED, chip_perm(chips, shared, shared))
    both = jnp.concatenate([mine, lax.ppermute(mine, LINKED, swap)], axis=0)
    fetched = [lax.ppermute(both, LINKED, chip_perm(chips, *pair)) for pair in pairs]
    early_weights = pl.pallas_call(
        functools.partial(early_kernel, per_block),
        out_shape=pltpu.VMEM((early, expert_hidden, width), jnp.bfloat16),
        in_specs=[pl.BlockSpec(memory_space=pl.ANY)] + [HBM] * 3,
        out_specs=VMEM,
        scratch_shapes=[pltpu.SemaphoreType.DMA((early,))],
        compiler_params=pltpu.CompilerParams(vmem_limit_bytes=VMEM_BYTES - early * chunk_bytes - 20 * 2**20),
        cost_estimate=pl.CostEstimate(flops=0, bytes_accessed=2 * early * chunk_bytes, transcendentals=0),
        name="early_weights",
    )(both, gate_weight, up_weight, down_weight)
    passed = [lax.ppermute(rows, LINKED, swap) for rows in fetched]
    shared_passed = lax.ppermute(shared_rows, LINKED, swap)
    pieces = [in_vmem(piece) for piece in [both] + fetched + passed + [shared_rows, shared_passed]]

    scratch_bytes = all_rows * width * (2 + 4 + 2 + 2 + 1) + all_rows * (width // parts + 5 * per_block * expert_hidden) * 4
    slots = min(RING_CHUNKS, chunks - early, (VMEM_BYTES - early * chunk_bytes - scratch_bytes - 6 * 2**20) // chunk_bytes)
    own, kept, sent = pl.pallas_call(
        functools.partial(expert_kernel, len(pieces), per_block, experts, parts),
        out_shape=(
            jax.ShapeDtypeStruct((chip_rows, width), jnp.float32),
            jax.ShapeDtypeStruct((reduced, width), jnp.float32),
            jax.ShapeDtypeStruct((reduced, width), jnp.bfloat16),
        ),
        in_specs=[VMEM] * (len(pieces) + 1) + [HBM] * 3,
        out_specs=(VMEM, VMEM, VMEM),
        scratch_shapes=[
            pltpu.VMEM((all_rows, width), jnp.bfloat16),
            pltpu.VMEM((all_rows, width), jnp.float32),
            pltpu.VMEM((slots, expert_hidden, width), jnp.bfloat16),
            pltpu.SemaphoreType.DMA((slots,)),
        ],
        compiler_params=pltpu.CompilerParams(vmem_limit_bytes=scratch_bytes + slots * chunk_bytes + 3 * 2**20),
        cost_estimate=pl.CostEstimate(
            flops=6 * all_rows * local_experts * expert_hidden * width,
            bytes_accessed=chunks * chunk_bytes,
            transcendentals=all_rows * local_experts * expert_hidden,
        ),
        name="experts",
    )(*pieces, early_weights, gate_weight, up_weight, down_weight)

    summed = call(
        chip_sum_kernel,
        [jax.ShapeDtypeStruct((chip_rows, width), jnp.bfloat16)] * len(pairs)
        + [jax.ShapeDtypeStruct((own_rows, width), jnp.bfloat16)],
        in_vmem(kept),
        in_vmem(lax.ppermute(sent, LINKED, swap)),
        name="chip_sum",
    )
    returned = [lax.ppermute(rows, LINKED, chip_perm(chips, *pair)) for rows, pair in zip(summed, pairs)]
    shared_back = lax.ppermute(summed[-1], LINKED, chip_perm(chips, shared, shared))
    half = jax.ShapeDtypeStruct((own_rows, width), jnp.float32)
    own_part, other_part = call(
        token_sum_kernel,
        [half, half],
        *[in_vmem(array) for array in [own, shared_back] + returned],
        name="token_sum",
    )
    return call(
        last_kernel,
        jax.ShapeDtypeStruct((own_rows, width), jnp.bfloat16),
        own_part,
        lax.ppermute(other_part, LINKED, swap),
        name="last_sum",
    )


def solution(mesh):
    by_device = P(("groups", "expert", "rep"), None)
    by_expert = P("expert", "rep", None)
    return jax.shard_map(
        local,
        mesh=mesh,
        in_specs=(by_device,) * 3 + (by_expert,) * 3,
        out_specs=by_device,
        check_vma=False,
    )
```

time: 214 us -> 56.1 us (0.26)
  waiting for transfers between devices: 100 us -> 12.7 us
  matrix products: 45.9 us -> 0 us
  Pallas kernels: 0 us -> 27.4 us
  blocking collectives: 26.3 us -> 0 us
  local copies, waits for them, and re-layouts: 15.1 us -> 0 us
  between operations: 13.6 us -> 0.09 us
  starting transfers between devices: 8.29 us -> 14.8 us
  other arithmetic: 3.86 us -> 0.8 us
    all_to_all x2 -> x0, waiting for transfers between devices: 72.7 us -> none  [the longest x1 36.6 us: local(): lax.all_to_all(partials, 'rep', split_axis=2, concat_axis=2, tiled=True)]
    dot_general x4 -> x0, matrix products: 45.9 us -> none  [the longest x1 16.7 us: expert_block(): jnp.einsum('sjncd,jhd->sjnch', block_rows, up_weight, preferred_element_t...]
    all_gather x1 -> x0, waiting for transfers between devices: 27.8 us -> none  [local(): lax.all_gather(arrived, 'rep', axis=2, tiled=True)]
    pallas_call x0 -> x6, Pallas kernels: none -> 27.4 us  [the longest x1 19.5 us: local(): pl.pallas_call(functools.partial(expert_kernel, len(pieces), per_block, e...]
    all_to_all x1 -> x0, blocking collectives: 26.3 us -> none  [local(): lax.all_to_all(outgoing, 'expert', split_axis=0, concat_axis=0, tiled=True)]
    ppermute x0 -> x15, starting transfers between devices: none -> 14.8 us  [the longest x3 6.72 us: local(): lax.ppermute(both, LINKED, chip_perm(chips, *pair))]
    ppermute x0 -> x15, waiting for transfers between devices: none -> 12.7 us  [the longest x3 5.25 us: local(): lax.ppermute(both, LINKED, chip_perm(chips, *pair))]
    all_to_all x2 -> x0, starting transfers between devices: 8.29 us -> none  [the longest x1 4.59 us: local(): lax.all_to_all(summed, 'expert', split_axis=0, concat_axis=0, tiled=True)]
  transfers between devices with their start and end apart: 3 -> 15, of which waited for: 3 -> 7; matrix products, arithmetic and copies ran while one was open for 0% -> 0% of each run, Pallas kernels for 0% -> 10%
where the time goes in v1:
time: 56.1 us; the launch traced here: 55.8 us
  Pallas kernels  27.4 us (49%)
  starting transfers between devices  14.8 us (26%)
  waiting for transfers between devices  12.7 us (23%)
  other arithmetic  0.8 us (1%)
    pallas_call x1, Pallas kernels, local(): pl.pallas_call(functools.partial(expert_kernel, len(pieces), per_block, e...  19.5 us
    ppermute x3, starting transfers between devices, local(): lax.ppermute(both, LINKED, chip_perm(chips, *pair))  6.72 us
    pallas_call x1, Pallas kernels, local(): pl.pallas_call(functools.partial(early_kernel, per_block), out_shape=pltp...  5.59 us
    ppermute x3, waiting for transfers between devices, local(): lax.ppermute(both, LINKED, chip_perm(chips, *pair))  5.25 us
    ppermute x3, starting transfers between devices, local(): lax.ppermute(rows, LINKED, chip_perm(chips, *pair))  5.09 us
    ppermute x1, waiting for transfers between devices, local(): lax.ppermute(summed[-1], LINKED, chip_perm(chips, shared, shared))  3.21 us
    pallas_call x1, Pallas kernels, local(): pl.pallas_call(functools.partial(rows_kernel, experts), out_shape=jax.Sha...  1.61 us
    ppermute x1, waiting for transfers between devices, local(): lax.ppermute(sent, LINKED, swap)  1.52 us
  transfers between devices with their start and end apart: 15, of which 7 were waited for; matrix products, arithmetic and copies ran while one was open for 0% of the time, Pallas kernels for 10%

profile of v1, /device:TPU:0, one launch (start us, length us, event | category | flops | bytes accessed | tf_op | source)
XLA Modules:
  0.0 55.8 jit_solution(15313672470527014802)
XLA Ops:
  0.0 1.6 %rows.1 = bf16[4,4224]{1,0:T(4,128)(2,1)} custom-call(bf16[4,4096]{1,0:T(4,128)(2,1)} %tokens_in.1, s32[4,8]{1,0:T(4,128)} %ids_in.1, f32[4,8]{1,0:T(4,128)} %probs_in.1), custom_call_target="tpu_custom_call" | custom-call | tf_op jit(solution)/shard_map/rows/pallas_call | solution.py:240
  1.6 0.5 collective-permute-start
  2.1 1.1 %collective-permute-done = bf16[4,4224]{1,0:T(4,128)(2,1)S(1)} collective-permute-done((bf16[4,4224]{1,0:T(4,128)(2,1)}, bf16[4,4224]{1,0:T(4,128)(2,1)S(1)}, u32[]{:S(2)}, u32[]{:S(2)}) %collective-permute-start) | collective-permute-done | bytes 33824 | tf_op jit(solution)/shard_map/ppermute | solution.py:251
  3.2 0.8 %pad_maximum_fusion.after_ref.refs_0_ = bf16[8,4224]{1,0:T(8,128)(2,1)S(1)} fusion(bf16[4,4224]{1,0:T(4,128)(2,1)S(1)} %collective-permute-done, bf16[4,4224]{1,0:T(4,128)(2,1)} %rows.1), kind=kLoop, calls=%fused_computation | loop fusion | flops 135168 | bytes 135168 | tf_op jit(solution)/shard_map/concatenate | solution.py:251
  4.0 3.0 %collective-permute-start.3 = (bf16[8,4224]{1,0:T(8,128)(2,1)S(1)}, bf16[8,4224]{1,0:T(8,128)(2,1)S(1)}, u32[]{:S(2)}, u32[]{:S(2)}) collective-permute-start(bf16[8,4224]{1,0:T(8,128)(2,1)S(1)} %pad_maximum_fusion.after_ref.refs_0_), channel_id=1, source_target_pairs={{0,4},{1,7},{2,6},{3,5},{4,0},{5,3},{6,2},{7,1},{8,12},{9,15},{10,... | collective-permute-start | bytes 202760 | tf_op jit(solution)/shard_map/ppermute | solution.py:252
  7.0 2.6 %collective-permute-start.2 = (bf16[8,4224]{1,0:T(8,128)(2,1)S(1)}, bf16[8,4224]{1,0:T(8,128)(2,1)S(1)}, u32[]{:S(2)}, u32[]{:S(2)}) collective-permute-start(bf16[8,4224]{1,0:T(8,128)(2,1)S(1)} %pad_maximum_fusion.after_ref.refs_0_), channel_id=1, source_target_pairs={{0,8},{1,11},{2,10},{3,9},{4,12},{5,15},{6,14},{7,13},{8,0},{9,3},... | collective-permute-start | bytes 202760 | tf_op jit(solution)/shard_map/ppermute | solution.py:252
  9.6 1.1 %collective-permute-start.1 = (bf16[8,4224]{1,0:T(8,128)(2,1)S(1)}, bf16[8,4224]{1,0:T(8,128)(2,1)S(1)}, u32[]{:S(2)}, u32[]{:S(2)}) collective-permute-start(bf16[8,4224]{1,0:T(8,128)(2,1)S(1)} %pad_maximum_fusion.after_ref.refs_0_), channel_id=1, source_target_pairs={{0,14},{1,13},{2,12},{3,15},{4,10},{5,9},{6,8},{7,11},{8,6},{9,5},... | collective-permute-start | bytes 202760 | tf_op jit(solution)/shard_map/ppermute | solution.py:252
  10.7 0.3 collective-permute-start.7
  11.1 0.0 collective-permute-done.3.refs_3_
  11.1 0.2 collective-permute-start.6
  11.3 3.0 %collective-permute-done.2.refs_2_ = bf16[8,4224]{1,0:T(8,128)(2,1)S(1)} collective-permute-done((bf16[8,4224]{1,0:T(8,128)(2,1)S(1)}, bf16[8,4224]{1,0:T(8,128)(2,1)S(1)}, u32[]{:S(2)}, u32[]{:S(2)}) %collective-permute-start.2) | collective-permute-done | bytes 67616 | tf_op jit(solution)/shard_map/ppermute | solution.py:252
  14.4 0.4 collective-permute-start.5
  14.8 2.2 %collective-permute-done.1.refs_1_ = bf16[8,4224]{1,0:T(8,128)(2,1)S(1)} collective-permute-done((bf16[8,4224]{1,0:T(8,128)(2,1)S(1)}, bf16[8,4224]{1,0:T(8,128)(2,1)S(1)}, u32[]{:S(2)}, u32[]{:S(2)}) %collective-permute-start.1) | collective-permute-done | bytes 67616 | tf_op jit(solution)/shard_map/ppermute | solution.py:252
  17.0 0.0 collective-permute-start.4
  17.0 0.0 collective-permute-done.7.refs_7_
  17.0 0.5 collective-permute-start.8
  17.5 5.6 %early_weights.1.refs_9_ = bf16[5,384,4096]{2,1,0:T(8,128)(2,1)S(1)} custom-call(bf16[8,4224]{1,0:T(8,128)(2,1)S(1)} %pad_maximum_fusion.after_ref.refs_0_, bf16[8,384,4096]{2,1,0:T(8,128)(2,1)} %refs_10_.1, bf16[8,384,4096]{2,1,0:T(8,128)(2,1)} %refs_11_.1, bf16[8,384,4096]{2,1,0:T(8,128)(2,1)} %refs_12_.1), custom_call_target="tpu_custom_call" | custom-call | bytes 31457280 | tf_op jit(solution)/shard_map/early_weights/pallas_call | solution.py:253
  23.1 0.0 collective-permute-done.8.refs_8_
  23.1 0.0 collective-permute-done.6.refs_6_
  23.1 0.0 collective-permute-done.5.refs_5_
  23.1 0.0 collective-permute-done.4.refs_4_
  23.1 19.5 %experts.1 = (f32[8,4096]{1,0:T(8,128)S(1)}, f32[32,4096]{1,0:T(8,128)S(1)}, bf16[32,4096]{1,0:T(8,128)(2,1)S(1)}) custom-call(bf16[8,4224]{1,0:T(8,128)(2,1)S(1)} %pad_maximum_fusion.after_ref.refs_0_, bf16[8,4224]{1,0:T(8,128)(2,1)S(1)} %collective-permute-done.1.refs_1_, bf16[8,4224]{1,0:T(8,128)(2,1)S(1)} %collective-permute-done.2.refs_2_, ...), custom_call_target="tpu_custom_call" | custom-call | flops 4831838208 | bytes 75497472 | tf_op jit(solution)/shard_map/experts/pallas_call | solution.py:269
  42.6 0.1 collective-permute-start.9
  42.7 1.5 %collective-permute-done.9.arrived_ref = bf16[32,4096]{1,0:T(8,128)(2,1)S(1)} collective-permute-done((bf16[32,4096]{1,0:T(8,128)(2,1)S(1)}, bf16[32,4096]{1,0:T(8,128)(2,1)S(1)}, u32[]{:S(2)}, u32[]{:S(2)}) %collective-permute-start.9) | collective-permute-done | bytes 262176 | tf_op jit(solution)/shard_map/ppermute | solution.py:298
  44.2 0.1 chip_sum.1
  44.3 2.4 %collective-permute-start.11 = (bf16[8,4096]{1,0:T(8,128)(2,1)S(1)}, bf16[8,4096]{1,0:T(8,128)(2,1)S(1)}, u32[]{:S(2)}, u32[]{:S(2)}) collective-permute-start(bf16[8,4096]{1,0:T(8,128)(2,1)S(1)} %get-tuple-element.18), channel_id=1, source_target_pairs={{0,14},{1,13},{2,12},{3,15},{4,10},{5,9},{6,8},{7,11},{8,6},{9,5},... | collective-permute-start | bytes 196616 | tf_op jit(solution)/shard_map/ppermute | solution.py:301
  46.7 0.6 %collective-permute-start.12 = (bf16[8,4096]{1,0:T(8,128)(2,1)S(1)}, bf16[8,4096]{1,0:T(8,128)(2,1)S(1)}, u32[]{:S(2)}, u32[]{:S(2)}) collective-permute-start(bf16[8,4096]{1,0:T(8,128)(2,1)S(1)} %get-tuple-element.19), channel_id=1, source_target_pairs={{0,8},{1,11},{2,10},{3,9},{4,12},{5,15},{6,14},{7,13},{8,0},{9,3},... | collective-permute-start | bytes 196616 | tf_op jit(solution)/shard_map/ppermute | solution.py:301
  47.3 2.0 %collective-permute-start.13 = (bf16[8,4096]{1,0:T(8,128)(2,1)S(1)}, bf16[8,4096]{1,0:T(8,128)(2,1)S(1)}, u32[]{:S(2)}, u32[]{:S(2)}) collective-permute-start(bf16[8,4096]{1,0:T(8,128)(2,1)S(1)} %get-tuple-element.20), channel_id=1, source_target_pairs={{0,4},{1,7},{2,6},{3,5},{4,0},{5,3},{6,2},{7,1},{8,12},{9,15},{10,... | collective-permute-start | bytes 196616 | tf_op jit(solution)/shard_map/ppermute | solution.py:301
  49.4 0.8 %collective-permute-start.10 = (bf16[4,4096]{1,0:T(4,128)(2,1)S(1)}, bf16[4,4096]{1,0:T(4,128)(2,1)S(1)}, u32[]{:S(2)}, u32[]{:S(2)}) collective-permute-start(bf16[4,4096]{1,0:T(4,128)(2,1)S(1)} %get-tuple-element.17), channel_id=1, source_target_pairs={{0,2},{1,3},{2,0},{3,1},{4,6},{5,7},{6,4},{7,5},{8,10},{9,11},{10,... | collective-permute-start | bytes 98312 | tf_op jit(solution)/shard_map/ppermute | solution.py:302
  50.2 3.2 %collective-permute-done.10.shared_ref = bf16[4,4096]{1,0:T(4,128)(2,1)S(1)} collective-permute-done((bf16[4,4096]{1,0:T(4,128)(2,1)S(1)}, bf16[4,4096]{1,0:T(4,128)(2,1)S(1)}, u32[]{:S(2)}, u32[]{:S(2)}) %collective-permute-start.10) | collective-permute-done | bytes 32800 | tf_op jit(solution)/shard_map/ppermute | solution.py:302
  53.4 0.0 collective-permute-done.11.refs_0_
  53.4 0.4 collective-permute-done.12.refs_1_
  53.8 0.0 collective-permute-done.13.refs_2_
  53.9 0.1 collective-permute-start.14
  53.9 1.2 %collective-permute-done.14.other_ref = f32[4,4096]{1,0:T(4,128)S(1)} collective-permute-done((f32[4,4096]{1,0:T(4,128)S(1)}, f32[4,4096]{1,0:T(4,128)S(1)}, u32[]{:S(2)}, u32[]{:S(2)}) %collective-permute-start.14) | collective-permute-done | bytes 65568 | tf_op jit(solution)/shard_map/ppermute | solution.py:314
  55.2 0.6 %last_sum.1 = bf16[4,4096]{1,0:T(4,128)(2,1)} custom-call(f32[4,4096]{1,0:T(4,128)S(1)} %get-tuple-element.21.mine_ref, f32[4,4096]{1,0:T(4,128)S(1)} %collective-permute-done.14.other_ref), custom_call_target="tpu_custom_call" | custom-call | tf_op jit(solution)/shard_map/last_sum/pallas_call | solution.py:214
  (1 shorter events, 0.0 us)
Async XLA Ops:
  1.6 1.6 %collective-permute-start = (bf16[4,4224]{1,0:T(4,128)(2,1)}, bf16[4,4224]{1,0:T(4,128)(2,1)S(1)}, u32[]{:S(2)}, u32[]{:S(2)}) collective-permute-start(bf16[4,4224]{1,0:T(4,128)(2,1)} %rows.1), channel_id=1, source_target_pairs={{0,1},{1,0},{2,3},{3,2},{4,5},{5,4},{6,7},{7,6},{8,9},{9,8},{10,11... | collective-permute-start | bytes 101384 | tf_op jit(solution)/shard_map/ppermute | solution.py:251
  4.0 7.1 %collective-permute-start.3 = (bf16[8,4224]{1,0:T(8,128)(2,1)S(1)}, bf16[8,4224]{1,0:T(8,128)(2,1)S(1)}, u32[]{:S(2)}, u32[]{:S(2)}) collective-permute-start(bf16[8,4224]{1,0:T(8,128)(2,1)S(1)} %pad_maximum_fusion.after_ref.refs_0_), channel_id=1, source_target_pairs={{0,4},{1,7},{2,6},{3,5},{4,0},{5,3},{6,2},{7,1},{8,12},{9,15},{10,... | collective-permute-start | bytes 202760 | tf_op jit(solution)/shard_map/ppermute | solution.py:252
  7.0 7.4 %collective-permute-start.2 = (bf16[8,4224]{1,0:T(8,128)(2,1)S(1)}, bf16[8,4224]{1,0:T(8,128)(2,1)S(1)}, u32[]{:S(2)}, u32[]{:S(2)}) collective-permute-start(bf16[8,4224]{1,0:T(8,128)(2,1)S(1)} %pad_maximum_fusion.after_ref.refs_0_), channel_id=1, source_target_pairs={{0,8},{1,11},{2,10},{3,9},{4,12},{5,15},{6,14},{7,13},{8,0},{9,3},... | collective-permute-start | bytes 202760 | tf_op jit(solution)/shard_map/ppermute | solution.py:252
  9.6 7.4 %collective-permute-start.1 = (bf16[8,4224]{1,0:T(8,128)(2,1)S(1)}, bf16[8,4224]{1,0:T(8,128)(2,1)S(1)}, u32[]{:S(2)}, u32[]{:S(2)}) collective-permute-start(bf16[8,4224]{1,0:T(8,128)(2,1)S(1)} %pad_maximum_fusion.after_ref.refs_0_), channel_id=1, source_target_pairs={{0,14},{1,13},{2,12},{3,15},{4,10},{5,9},{6,8},{7,11},{8,6},{9,5},... | collective-permute-start | bytes 202760 | tf_op jit(solution)/shard_map/ppermute | solution.py:252
  10.7 6.2 %collective-permute-start.7 = (bf16[4,4224]{1,0:T(4,128)(2,1)}, bf16[4,4224]{1,0:T(4,128)(2,1)S(1)}, u32[]{:S(2)}, u32[]{:S(2)}) collective-permute-start(bf16[4,4224]{1,0:T(4,128)(2,1)} %rows.1), channel_id=1, source_target_pairs={{0,2},{1,3},{2,0},{3,1},{4,6},{5,7},{6,4},{7,5},{8,10},{9,11},{10,... | collective-permute-start | bytes 101384 | tf_op jit(solution)/shard_map/ppermute | solution.py:250
  11.1 12.0 %collective-permute-start.6 = (bf16[8,4224]{1,0:T(8,128)(2,1)S(1)}, bf16[8,4224]{1,0:T(8,128)(2,1)S(1)}, u32[]{:S(2)}, u32[]{:S(2)}) collective-permute-start(bf16[8,4224]{1,0:T(8,128)(2,1)S(1)} %collective-permute-done.3.refs_3_), channel_id=1, source_target_pairs={{0,1},{1,0},{2,3},{3,2},{4,5},{5,4},{6,7},{7,6},{8,9},{9,8},{10,11... | collective-permute-start | bytes 202760 | tf_op jit(solution)/shard_map/ppermute | solution.py:263
  14.4 8.7 %collective-permute-start.5 = (bf16[8,4224]{1,0:T(8,128)(2,1)S(1)}, bf16[8,4224]{1,0:T(8,128)(2,1)S(1)}, u32[]{:S(2)}, u32[]{:S(2)}) collective-permute-start(bf16[8,4224]{1,0:T(8,128)(2,1)S(1)} %collective-permute-done.2.refs_2_), channel_id=1, source_target_pairs={{0,1},{1,0},{2,3},{3,2},{4,5},{5,4},{6,7},{7,6},{8,9},{9,8},{10,11... | collective-permute-start | bytes 202760 | tf_op jit(solution)/shard_map/ppermute | solution.py:263
  17.0 6.1 %collective-permute-start.4 = (bf16[8,4224]{1,0:T(8,128)(2,1)S(1)}, bf16[8,4224]{1,0:T(8,128)(2,1)S(1)}, u32[]{:S(2)}, u32[]{:S(2)}) collective-permute-start(bf16[8,4224]{1,0:T(8,128)(2,1)S(1)} %collective-permute-done.1.refs_1_), channel_id=1, source_target_pairs={{0,1},{1,0},{2,3},{3,2},{4,5},{5,4},{6,7},{7,6},{8,9},{9,8},{10,11... | collective-permute-start | bytes 202760 | tf_op jit(solution)/shard_map/ppermute | solution.py:263
  17.0 6.1 %collective-permute-start.8 = (bf16[4,4224]{1,0:T(4,128)(2,1)S(1)}, bf16[4,4224]{1,0:T(4,128)(2,1)S(1)}, u32[]{:S(2)}, u32[]{:S(2)}) collective-permute-start(bf16[4,4224]{1,0:T(4,128)(2,1)S(1)} %collective-permute-done.7.refs_7_), channel_id=1, source_target_pairs={{0,1},{1,0},{2,3},{3,2},{4,5},{5,4},{6,7},{7,6},{8,9},{9,8},{10,11... | collective-permute-start | bytes 101384 | tf_op jit(solution)/shard_map/ppermute | solution.py:264
  42.6 1.6 %collective-permute-start.9 = (bf16[32,4096]{1,0:T(8,128)(2,1)S(1)}, bf16[32,4096]{1,0:T(8,128)(2,1)S(1)}, u32[]{:S(2)}, u32[]{:S(2)}) collective-permute-start(bf16[32,4096]{1,0:T(8,128)(2,1)S(1)} %get-tuple-element.16), channel_id=1, source_target_pairs={{0,1},{1,0},{2,3},{3,2},{4,5},{5,4},{6,7},{7,6},{8,9},{9,8},{10,11... | collective-permute-start | bytes 786440 | tf_op jit(solution)/shard_map/ppermute | solution.py:298
  44.3 9.1 %collective-permute-start.11 = (bf16[8,4096]{1,0:T(8,128)(2,1)S(1)}, bf16[8,4096]{1,0:T(8,128)(2,1)S(1)}, u32[]{:S(2)}, u32[]{:S(2)}) collective-permute-start(bf16[8,4096]{1,0:T(8,128)(2,1)S(1)} %get-tuple-element.18), channel_id=1, source_target_pairs={{0,14},{1,13},{2,12},{3,15},{4,10},{5,9},{6,8},{7,11},{8,6},{9,5},... | collective-permute-start | bytes 196616 | tf_op jit(solution)/shard_map/ppermute | solution.py:301
  46.7 7.1 %collective-permute-start.12 = (bf16[8,4096]{1,0:T(8,128)(2,1)S(1)}, bf16[8,4096]{1,0:T(8,128)(2,1)S(1)}, u32[]{:S(2)}, u32[]{:S(2)}) collective-permute-start(bf16[8,4096]{1,0:T(8,128)(2,1)S(1)} %get-tuple-element.19), channel_id=1, source_target_pairs={{0,8},{1,11},{2,10},{3,9},{4,12},{5,15},{6,14},{7,13},{8,0},{9,3},... | collective-permute-start | bytes 196616 | tf_op jit(solution)/shard_map/ppermute | solution.py:301
  47.3 6.5 %collective-permute-start.13 = (bf16[8,4096]{1,0:T(8,128)(2,1)S(1)}, bf16[8,4096]{1,0:T(8,128)(2,1)S(1)}, u32[]{:S(2)}, u32[]{:S(2)}) collective-permute-start(bf16[8,4096]{1,0:T(8,128)(2,1)S(1)} %get-tuple-element.20), channel_id=1, source_target_pairs={{0,4},{1,7},{2,6},{3,5},{4,0},{5,3},{6,2},{7,1},{8,12},{9,15},{10,... | collective-permute-start | bytes 196616 | tf_op jit(solution)/shard_map/ppermute | solution.py:301
  49.4 4.0 %collective-permute-start.10 = (bf16[4,4096]{1,0:T(4,128)(2,1)S(1)}, bf16[4,4096]{1,0:T(4,128)(2,1)S(1)}, u32[]{:S(2)}, u32[]{:S(2)}) collective-permute-start(bf16[4,4096]{1,0:T(4,128)(2,1)S(1)} %get-tuple-element.17), channel_id=1, source_target_pairs={{0,2},{1,3},{2,0},{3,1},{4,6},{5,7},{6,4},{7,5},{8,10},{9,11},{10,... | collective-permute-start | bytes 98312 | tf_op jit(solution)/shard_map/ppermute | solution.py:302
  53.9 1.3 %collective-permute-start.14 = (f32[4,4096]{1,0:T(4,128)S(1)}, f32[4,4096]{1,0:T(4,128)S(1)}, u32[]{:S(2)}, u32[]{:S(2)}) collective-permute-start(f32[4,4096]{1,0:T(4,128)S(1)} %get-tuple-element.22), channel_id=1, source_target_pairs={{0,1},{1,0},{2,3},{3,2},{4,5},{5,4},{6,7},{7,6},{8,9},{9,8},{10,11... | collective-permute-start | bytes 196616 | tf_op jit(solution)/shard_map/ppermute | solution.py:314

commit v2 on v1

--- a/solution.py
+++ b/solution.py
@@ -77,7 +77,7 @@
     return down_ref.at[block * per_block + place - 2 * per_block]
 
 
-def early_kernel(per_block, after_ref, gate_ref, up_ref, down_ref, early_ref, sem):
+def early_kernel(per_block, after_ref, gate_ref, up_ref, down_ref, early_ref, done_ref, sem):
     copies = [
         pltpu.make_async_copy(
             chunk_of((gate_ref, up_ref, down_ref), gate_ref.shape[0], per_block, index), early_ref.at[index], sem.at[index]
@@ -88,11 +88,12 @@
         copy.start()
     for copy in copies:
         copy.wait()
+    done_ref[...] = jnp.zeros_like(done_ref)
 
 
 def expert_kernel(pieces, per_block, experts, parts, *refs):
     row_refs = refs[:pieces]
-    early_ref, gate_ref, up_ref, down_ref, own_ref, kept_ref, sent_ref, rows, total, ring, ring_sem = refs[pieces:]
+    _, early_ref, gate_ref, up_ref, down_ref, own_ref, kept_ref, sent_ref, rows, total, ring, ring_sem = refs[pieces:]
     local_experts, expert_hidden, width = gate_ref.shape
     tokens = rows.shape[0]
     early, slots, chunks = early_ref.shape[0], ring.shape[0], 3 * local_experts
@@ -250,22 +251,27 @@
     shared_rows = lax.ppermute(mine, LINKED, chip_perm(chips, shared, shared))
     both = jnp.concatenate([mine, lax.ppermute(mine, LINKED, swap)], axis=0)
     fetched = [lax.ppermute(both, LINKED, chip_perm(chips, *pair)) for pair in pairs]
-    early_weights = pl.pallas_call(
+    scratch_bytes = all_rows * width * (2 + 4 + 2 + 2 + 1) + all_rows * (width // parts + 5 * per_block * expert_hidden) * 4
+    slots = min(RING_CHUNKS, chunks - early, (VMEM_BYTES - early * chunk_bytes - scratch_bytes - 6 * 2**20) // chunk_bytes)
+    vmem_limit_bytes = scratch_bytes + slots * chunk_bytes + 3 * 2**20
+    early_weights, early_done = pl.pallas_call(
         functools.partial(early_kernel, per_block),
-        out_shape=pltpu.VMEM((early, expert_hidden, width), jnp.bfloat16),
+        out_shape=(
+            pltpu.VMEM((early, expert_hidden, width), jnp.bfloat16),
+            jax.ShapeDtypeStruct((8, LANES), jnp.float32),
+        ),
         in_specs=[pl.BlockSpec(memory_space=pl.ANY)] + [HBM] * 3,
-        out_specs=VMEM,
+        out_specs=(VMEM, VMEM),
         scratch_shapes=[pltpu.SemaphoreType.DMA((early,))],
-        compiler_params=pltpu.CompilerParams(vmem_limit_bytes=VMEM_BYTES - early * chunk_bytes - 20 * 2**20),
+        compiler_params=pltpu.CompilerParams(vmem_limit_bytes=vmem_limit_bytes),
         cost_estimate=pl.CostEstimate(flops=0, bytes_accessed=2 * early * chunk_bytes, transcendentals=0),
         name="early_weights",
     )(both, gate_weight, up_weight, down_weight)
+    *fetched, early_done = lax.optimization_barrier((*fetched, early_done))
     passed = [lax.ppermute(rows, LINKED, swap) for rows in fetched]
     shared_passed = lax.ppermute(shared_rows, LINKED, swap)
     pieces = [in_vmem(piece) for piece in [both] + fetched + passed + [shared_rows, shared_passed]]
 
-    scratch_bytes = all_rows * width * (2 + 4 + 2 + 2 + 1) + all_rows * (width // parts + 5 * per_block * expert_hidden) * 4
-    slots = min(RING_CHUNKS, chunks - early, (VMEM_BYTES - early * chunk_bytes - scratch_bytes - 6 * 2**20) // chunk_bytes)
     own, kept, sent = pl.pallas_call(
         functools.partial(expert_kernel, len(pieces), per_block, experts, parts),
         out_shape=(
@@ -273,7 +279,7 @@
             jax.ShapeDtypeStruct((reduced, width), jnp.float32),
             jax.ShapeDtypeStruct((reduced, width), jnp.bfloat16),
         ),
-        in_specs=[VMEM] * (len(pieces) + 1) + [HBM] * 3,
+        in_specs=[VMEM] * len(pieces) + [pl.BlockSpec(memory_space=pl.ANY), VMEM] + [HBM] * 3,
         out_specs=(VMEM, VMEM, VMEM),
         scratch_shapes=[
             pltpu.VMEM((all_rows, width), jnp.bfloat16),
@@ -281,14 +287,14 @@
             pltpu.VMEM((slots, expert_hidden, width), jnp.bfloat16),
             pltpu.SemaphoreType.DMA((slots,)),
         ],
-        compiler_params=pltpu.CompilerParams(vmem_limit_bytes=scratch_bytes + slots * chunk_bytes + 3 * 2**20),
+        compiler_params=pltpu.CompilerParams(vmem_limit_bytes=vmem_limit_bytes),
         cost_estimate=pl.CostEstimate(
             flops=6 * all_rows * local_experts * expert_hidden * width,
             bytes_accessed=chunks * chunk_bytes,
             transcendentals=all_rows * local_experts * expert_hidden,
         ),
         name="experts",
-    )(*pieces, early_weights, gate_weight, up_weight, down_weight)
+    )(*pieces, early_done, early_weights, gate_weight, up_weight, down_weight)
 
     summed = call(
         chip_sum_kernel,

time: 56.1 us -> 52.6 us (0.938)
  waiting for transfers between devices: 12.7 us -> 9.05 us
    ppermute x3, waiting for transfers between devices: 5.25 us -> 0.26 us  [local(): lax.ppermute(both, LINKED, chip_perm(chips, *pair))]
    ppermute x1, waiting for transfers between devices: 0.01 us -> 0.86 us  [local(): shared_passed = lax.ppermute(shared_rows, LINKED, swap)]
  transfers between devices with their start and end apart: 15 -> 15, of which waited for: 7 -> 8; matrix products, arithmetic and copies ran while one was open for 0% -> 0% of each run, Pallas kernels for 10% -> 11%
where the time goes in v2:
time: 52.6 us; the launch traced here: 52.3 us
  Pallas kernels  27.4 us (52%)
  starting transfers between devices  15 us (29%)
  waiting for transfers between devices  9.05 us (17%)
  other arithmetic  0.8 us (2%)
    pallas_call x1, Pallas kernels, local(): pl.pallas_call(functools.partial(expert_kernel, len(pieces), per_block, e...  19.5 us
    ppermute x3, starting transfers between devices, local(): lax.ppermute(both, LINKED, chip_perm(chips, *pair))  6.72 us
    pallas_call x1, Pallas kernels, local(): pl.pallas_call(functools.partial(early_kernel, per_block), out_shape=(plt...  5.59 us
    ppermute x3, starting transfers between devices, local(): lax.ppermute(rows, LINKED, chip_perm(chips, *pair))  5.39 us
    ppermute x1, waiting for transfers between devices, local(): lax.ppermute(summed[-1], LINKED, chip_perm(chips, shared, shared))  3.73 us
    pallas_call x1, Pallas kernels, local(): pl.pallas_call(functools.partial(rows_kernel, experts), out_shape=jax.Sha...  1.63 us
    ppermute x1, waiting for transfers between devices, local(): lax.ppermute(other_part, LINKED, swap)  1.24 us
    ppermute x1, waiting for transfers between devices, local(): lax.ppermute(sent, LINKED, swap)  1.2 us
  transfers between devices with their start and end apart: 15, of which 8 were waited for; matrix products, arithmetic and copies ran while one was open for 0% of the time, Pallas kernels for 11%

profile of v2, /device:TPU:0, one launch (start us, length us, event | category | flops | bytes accessed | tf_op | source)
XLA Modules:
  0.0 52.3 jit_solution(4634571655133551939)
XLA Ops:
  0.0 1.6 %rows.1 = bf16[4,4224]{1,0:T(4,128)(2,1)} custom-call(bf16[4,4096]{1,0:T(4,128)(2,1)} %tokens_in.1, s32[4,8]{1,0:T(4,128)} %ids_in.1, f32[4,8]{1,0:T(4,128)} %probs_in.1), custom_call_target="tpu_custom_call" | custom-call | tf_op jit(solution)/shard_map/rows/pallas_call | solution.py:241
  1.6 0.5 collective-permute-start
  2.2 1.1 %collective-permute-done = bf16[4,4224]{1,0:T(4,128)(2,1)S(1)} collective-permute-done((bf16[4,4224]{1,0:T(4,128)(2,1)}, bf16[4,4224]{1,0:T(4,128)(2,1)S(1)}, u32[]{:S(2)}, u32[]{:S(2)}) %collective-permute-start) | collective-permute-done | bytes 33824 | tf_op jit(solution)/shard_map/ppermute | solution.py:252
  3.2 0.8 %pad_maximum_fusion.after_ref.refs_0_ = bf16[8,4224]{1,0:T(8,128)(2,1)S(1)} fusion(bf16[4,4224]{1,0:T(4,128)(2,1)S(1)} %collective-permute-done, bf16[4,4224]{1,0:T(4,128)(2,1)} %rows.1), kind=kLoop, calls=%fused_computation | loop fusion | flops 135168 | bytes 135168 | tf_op jit(solution)/shard_map/concatenate | solution.py:252
  4.0 3.0 %collective-permute-start.3 = (bf16[8,4224]{1,0:T(8,128)(2,1)S(1)}, bf16[8,4224]{1,0:T(8,128)(2,1)S(1)}, u32[]{:S(2)}, u32[]{:S(2)}) collective-permute-start(bf16[8,4224]{1,0:T(8,128)(2,1)S(1)} %pad_maximum_fusion.after_ref.refs_0_), channel_id=1, source_target_pairs={{0,4},{1,7},{2,6},{3,5},{4,0},{5,3},{6,2},{7,1},{8,12},{9,15},{10,... | collective-permute-start | bytes 202760 | tf_op jit(solution)/shard_map/ppermute | solution.py:253
  7.0 2.6 %collective-permute-start.2 = (bf16[8,4224]{1,0:T(8,128)(2,1)S(1)}, bf16[8,4224]{1,0:T(8,128)(2,1)S(1)}, u32[]{:S(2)}, u32[]{:S(2)}) collective-permute-start(bf16[8,4224]{1,0:T(8,128)(2,1)S(1)} %pad_maximum_fusion.after_ref.refs_0_), channel_id=1, source_target_pairs={{0,8},{1,11},{2,10},{3,9},{4,12},{5,15},{6,14},{7,13},{8,0},{9,3},... | collective-permute-start | bytes 202760 | tf_op jit(solution)/shard_map/ppermute | solution.py:253
  9.6 1.1 %collective-permute-start.1 = (bf16[8,4224]{1,0:T(8,128)(2,1)S(1)}, bf16[8,4224]{1,0:T(8,128)(2,1)S(1)}, u32[]{:S(2)}, u32[]{:S(2)}) collective-permute-start(bf16[8,4224]{1,0:T(8,128)(2,1)S(1)} %pad_maximum_fusion.after_ref.refs_0_), channel_id=1, source_target_pairs={{0,14},{1,13},{2,12},{3,15},{4,10},{5,9},{6,8},{7,11},{8,6},{9,5},... | collective-permute-start | bytes 202760 | tf_op jit(solution)/shard_map/ppermute | solution.py:253
  10.7 0.3 collective-permute-start.7
  11.1 5.6 %early_weights.1 = (bf16[5,384,4096]{2,1,0:T(8,128)(2,1)S(1)}, f32[8,128]{1,0:T(8,128)S(1)}) custom-call(bf16[8,4224]{1,0:T(8,128)(2,1)S(1)} %pad_maximum_fusion.after_ref.refs_0_, bf16[8,384,4096]{2,1,0:T(8,128)(2,1)} %refs_11_.1, bf16[8,384,4096]{2,1,0:T(8,128)(2,1)} %refs_12_.1, bf16[8,384,4096]{2,1,0:T(8,128)(2,1)} %refs_13_.1), custom_call_target="tpu_custom_call" | custom-call | bytes 31457280 | tf_op jit(solution)/shard_map/early_weights/pallas_call | solution.py:257
  16.7 0.0 collective-permute-done.3.refs_3_
  16.7 0.0 collective-permute-done.2.refs_2_
  16.7 0.3 collective-permute-done.1.refs_1_
  17.0 0.0 collective-permute-start.4
  17.0 0.5 collective-permute-start.5
  17.5 0.0 collective-permute-start.6
  17.5 0.0 collective-permute-done.7.refs_7_
  17.5 0.5 collective-permute-start.8
  18.0 0.9 %collective-permute-done.8.refs_8_ = bf16[4,4224]{1,0:T(4,128)(2,1)S(1)} collective-permute-done((bf16[4,4224]{1,0:T(4,128)(2,1)S(1)}, bf16[4,4224]{1,0:T(4,128)(2,1)S(1)}, u32[]{:S(2)}, u32[]{:S(2)}) %collective-permute-start.8) | collective-permute-done | bytes 33824 | tf_op jit(solution)/shard_map/ppermute | solution.py:272
  18.9 0.0 collective-permute-done.4.refs_4_
  18.9 0.0 collective-permute-done.5.refs_5_
  18.9 0.0 collective-permute-done.6.refs_6_
  18.9 19.5 %experts.1 = (f32[8,4096]{1,0:T(8,128)S(1)}, f32[32,4096]{1,0:T(8,128)S(1)}, bf16[32,4096]{1,0:T(8,128)(2,1)S(1)}) custom-call(bf16[8,4224]{1,0:T(8,128)(2,1)S(1)} %pad_maximum_fusion.after_ref.refs_0_, bf16[8,4224]{1,0:T(8,128)(2,1)S(1)} %collective-permute-done.1.refs_1_, bf16[8,4224]{1,0:T(8,128)(2,1)S(1)} %collective-permute-done.2.refs_2_, ...), custom_call_target="tpu_custom_call" | custom-call | flops 4831838208 | bytes 75497472 | tf_op jit(solution)/shard_map/experts/pallas_call | solution.py:275
  38.3 0.4 collective-permute-start.9
  38.8 1.2 %collective-permute-done.9.arrived_ref = bf16[32,4096]{1,0:T(8,128)(2,1)S(1)} collective-permute-done((bf16[32,4096]{1,0:T(8,128)(2,1)S(1)}, bf16[32,4096]{1,0:T(8,128)(2,1)S(1)}, u32[]{:S(2)}, u32[]{:S(2)}) %collective-permute-start.9) | collective-permute-done | bytes 262176 | tf_op jit(solution)/shard_map/ppermute | solution.py:304
  39.9 0.1 chip_sum.1
  40.0 4.6 %collective-permute-start.11 = (bf16[8,4096]{1,0:T(8,128)(2,1)S(1)}, bf16[8,4096]{1,0:T(8,128)(2,1)S(1)}, u32[]{:S(2)}, u32[]{:S(2)}) collective-permute-start(bf16[8,4096]{1,0:T(8,128)(2,1)S(1)} %get-tuple-element.30), channel_id=1, source_target_pairs={{0,14},{1,13},{2,12},{3,15},{4,10},{5,9},{6,8},{7,11},{8,6},{9,5},... | collective-permute-start | bytes 196616 | tf_op jit(solution)/shard_map/ppermute | solution.py:307
  44.6 0.0 collective-permute-start.12
  44.6 0.8 %collective-permute-start.13 = (bf16[8,4096]{1,0:T(8,128)(2,1)S(1)}, bf16[8,4096]{1,0:T(8,128)(2,1)S(1)}, u32[]{:S(2)}, u32[]{:S(2)}) collective-permute-start(bf16[8,4096]{1,0:T(8,128)(2,1)S(1)} %get-tuple-element.32), channel_id=1, source_target_pairs={{0,4},{1,7},{2,6},{3,5},{4,0},{5,3},{6,2},{7,1},{8,12},{9,15},{10,... | collective-permute-start | bytes 196616 | tf_op jit(solution)/shard_map/ppermute | solution.py:307
  45.4 0.5 %collective-permute-start.10 = (bf16[4,4096]{1,0:T(4,128)(2,1)S(1)}, bf16[4,4096]{1,0:T(4,128)(2,1)S(1)}, u32[]{:S(2)}, u32[]{:S(2)}) collective-permute-start(bf16[4,4096]{1,0:T(4,128)(2,1)S(1)} %get-tuple-element.29), channel_id=1, source_target_pairs={{0,2},{1,3},{2,0},{3,1},{4,6},{5,7},{6,4},{7,5},{8,10},{9,11},{10,... | collective-permute-start | bytes 98312 | tf_op jit(solution)/shard_map/ppermute | solution.py:308
  45.9 3.7 %collective-permute-done.10.shared_ref = bf16[4,4096]{1,0:T(4,128)(2,1)S(1)} collective-permute-done((bf16[4,4096]{1,0:T(4,128)(2,1)S(1)}, bf16[4,4096]{1,0:T(4,128)(2,1)S(1)}, u32[]{:S(2)}, u32[]{:S(2)}) %collective-permute-start.10) | collective-permute-done | bytes 32800 | tf_op jit(solution)/shard_map/ppermute | solution.py:308
  49.7 0.0 collective-permute-done.11.refs_0_
  49.7 0.2 collective-permute-done.12.refs_1_
  49.9 0.5 collective-permute-done.13.refs_2_
  50.4 0.1 collective-permute-start.14
  50.5 1.2 %collective-permute-done.14.other_ref = f32[4,4096]{1,0:T(4,128)S(1)} collective-permute-done((f32[4,4096]{1,0:T(4,128)S(1)}, f32[4,4096]{1,0:T(4,128)S(1)}, u32[]{:S(2)}, u32[]{:S(2)}) %collective-permute-start.14) | collective-permute-done | bytes 65568 | tf_op jit(solution)/shard_map/ppermute | solution.py:320
  51.7 0.6 %last_sum.1 = bf16[4,4096]{1,0:T(4,128)(2,1)} custom-call(f32[4,4096]{1,0:T(4,128)S(1)} %get-tuple-element.33.mine_ref, f32[4,4096]{1,0:T(4,128)S(1)} %collective-permute-done.14.other_ref), custom_call_target="tpu_custom_call" | custom-call | tf_op jit(solution)/shard_map/last_sum/pallas_call | solution.py:215
  (1 shorter events, 0.0 us)
Async XLA Ops:
  1.6 1.6 %collective-permute-start = (bf16[4,4224]{1,0:T(4,128)(2,1)}, bf16[4,4224]{1,0:T(4,128)(2,1)S(1)}, u32[]{:S(2)}, u32[]{:S(2)}) collective-permute-start(bf16[4,4224]{1,0:T(4,128)(2,1)} %rows.1), channel_id=1, source_target_pairs={{0,1},{1,0},{2,3},{3,2},{4,5},{5,4},{6,7},{7,6},{8,9},{9,8},{10,11... | collective-permute-start | bytes 101384 | tf_op jit(solution)/shard_map/ppermute | solution.py:252
  4.0 12.7 %collective-permute-start.3 = (bf16[8,4224]{1,0:T(8,128)(2,1)S(1)}, bf16[8,4224]{1,0:T(8,128)(2,1)S(1)}, u32[]{:S(2)}, u32[]{:S(2)}) collective-permute-start(bf16[8,4224]{1,0:T(8,128)(2,1)S(1)} %pad_maximum_fusion.after_ref.refs_0_), channel_id=1, source_target_pairs={{0,4},{1,7},{2,6},{3,5},{4,0},{5,3},{6,2},{7,1},{8,12},{9,15},{10,... | collective-permute-start | bytes 202760 | tf_op jit(solution)/shard_map/ppermute | solution.py:253
  7.0 9.7 %collective-permute-start.2 = (bf16[8,4224]{1,0:T(8,128)(2,1)S(1)}, bf16[8,4224]{1,0:T(8,128)(2,1)S(1)}, u32[]{:S(2)}, u32[]{:S(2)}) collective-permute-start(bf16[8,4224]{1,0:T(8,128)(2,1)S(1)} %pad_maximum_fusion.after_ref.refs_0_), channel_id=1, source_target_pairs={{0,8},{1,11},{2,10},{3,9},{4,12},{5,15},{6,14},{7,13},{8,0},{9,3},... | collective-permute-start | bytes 202760 | tf_op jit(solution)/shard_map/ppermute | solution.py:253
  9.6 7.4 %collective-permute-start.1 = (bf16[8,4224]{1,0:T(8,128)(2,1)S(1)}, bf16[8,4224]{1,0:T(8,128)(2,1)S(1)}, u32[]{:S(2)}, u32[]{:S(2)}) collective-permute-start(bf16[8,4224]{1,0:T(8,128)(2,1)S(1)} %pad_maximum_fusion.after_ref.refs_0_), channel_id=1, source_target_pairs={{0,14},{1,13},{2,12},{3,15},{4,10},{5,9},{6,8},{7,11},{8,6},{9,5},... | collective-permute-start | bytes 202760 | tf_op jit(solution)/shard_map/ppermute | solution.py:253
  10.7 6.8 %collective-permute-start.7 = (bf16[4,4224]{1,0:T(4,128)(2,1)}, bf16[4,4224]{1,0:T(4,128)(2,1)S(1)}, u32[]{:S(2)}, u32[]{:S(2)}) collective-permute-start(bf16[4,4224]{1,0:T(4,128)(2,1)} %rows.1), channel_id=1, source_target_pairs={{0,2},{1,3},{2,0},{3,1},{4,6},{5,7},{6,4},{7,5},{8,10},{9,11},{10,... | collective-permute-start | bytes 101384 | tf_op jit(solution)/shard_map/ppermute | solution.py:251
  17.0 1.9 %collective-permute-start.4 = (bf16[8,4224]{1,0:T(8,128)(2,1)S(1)}, bf16[8,4224]{1,0:T(8,128)(2,1)S(1)}, u32[]{:S(2)}, u32[]{:S(2)}) collective-permute-start(bf16[8,4224]{1,0:T(8,128)(2,1)S(1)} %collective-permute-done.1.refs_1_), channel_id=1, source_target_pairs={{0,1},{1,0},{2,3},{3,2},{4,5},{5,4},{6,7},{7,6},{8,9},{9,8},{10,11... | collective-permute-start | bytes 202760 | tf_op jit(solution)/shard_map/ppermute | solution.py:271
  17.0 1.9 %collective-permute-start.5 = (bf16[8,4224]{1,0:T(8,128)(2,1)S(1)}, bf16[8,4224]{1,0:T(8,128)(2,1)S(1)}, u32[]{:S(2)}, u32[]{:S(2)}) collective-permute-start(bf16[8,4224]{1,0:T(8,128)(2,1)S(1)} %collective-permute-done.2.refs_2_), channel_id=1, source_target_pairs={{0,1},{1,0},{2,3},{3,2},{4,5},{5,4},{6,7},{7,6},{8,9},{9,8},{10,11... | collective-permute-start | bytes 202760 | tf_op jit(solution)/shard_map/ppermute | solution.py:271
  17.5 1.4 %collective-permute-start.6 = (bf16[8,4224]{1,0:T(8,128)(2,1)S(1)}, bf16[8,4224]{1,0:T(8,128)(2,1)S(1)}, u32[]{:S(2)}, u32[]{:S(2)}) collective-permute-start(bf16[8,4224]{1,0:T(8,128)(2,1)S(1)} %collective-permute-done.3.refs_3_), channel_id=1, source_target_pairs={{0,1},{1,0},{2,3},{3,2},{4,5},{5,4},{6,7},{7,6},{8,9},{9,8},{10,11... | collective-permute-start | bytes 202760 | tf_op jit(solution)/shard_map/ppermute | solution.py:271
  17.5 1.3 %collective-permute-start.8 = (bf16[4,4224]{1,0:T(4,128)(2,1)S(1)}, bf16[4,4224]{1,0:T(4,128)(2,1)S(1)}, u32[]{:S(2)}, u32[]{:S(2)}) collective-permute-start(bf16[4,4224]{1,0:T(4,128)(2,1)S(1)} %collective-permute-done.7.refs_7_), channel_id=1, source_target_pairs={{0,1},{1,0},{2,3},{3,2},{4,5},{5,4},{6,7},{7,6},{8,9},{9,8},{10,11... | collective-permute-start | bytes 101384 | tf_op jit(solution)/shard_map/ppermute | solution.py:272
  38.3 1.6 %collective-permute-start.9 = (bf16[32,4096]{1,0:T(8,128)(2,1)S(1)}, bf16[32,4096]{1,0:T(8,128)(2,1)S(1)}, u32[]{:S(2)}, u32[]{:S(2)}) collective-permute-start(bf16[32,4096]{1,0:T(8,128)(2,1)S(1)} %get-tuple-element.28), channel_id=1, source_target_pairs={{0,1},{1,0},{2,3},{3,2},{4,5},{5,4},{6,7},{7,6},{8,9},{9,8},{10,11... | collective-permute-start | bytes 786440 | tf_op jit(solution)/shard_map/ppermute | solution.py:304
  40.0 9.7 %collective-permute-start.11 = (bf16[8,4096]{1,0:T(8,128)(2,1)S(1)}, bf16[8,4096]{1,0:T(8,128)(2,1)S(1)}, u32[]{:S(2)}, u32[]{:S(2)}) collective-permute-start(bf16[8,4096]{1,0:T(8,128)(2,1)S(1)} %get-tuple-element.30), channel_id=1, source_target_pairs={{0,14},{1,13},{2,12},{3,15},{4,10},{5,9},{6,8},{7,11},{8,6},{9,5},... | collective-permute-start | bytes 196616 | tf_op jit(solution)/shard_map/ppermute | solution.py:307
  44.6 5.3 %collective-permute-start.12 = (bf16[8,4096]{1,0:T(8,128)(2,1)S(1)}, bf16[8,4096]{1,0:T(8,128)(2,1)S(1)}, u32[]{:S(2)}, u32[]{:S(2)}) collective-permute-start(bf16[8,4096]{1,0:T(8,128)(2,1)S(1)} %get-tuple-element.31), channel_id=1, source_target_pairs={{0,8},{1,11},{2,10},{3,9},{4,12},{5,15},{6,14},{7,13},{8,0},{9,3},... | collective-permute-start | bytes 196616 | tf_op jit(solution)/shard_map/ppermute | solution.py:307
  44.6 5.7 %collective-permute-start.13 = (bf16[8,4096]{1,0:T(8,128)(2,1)S(1)}, bf16[8,4096]{1,0:T(8,128)(2,1)S(1)}, u32[]{:S(2)}, u32[]{:S(2)}) collective-permute-start(bf16[8,4096]{1,0:T(8,128)(2,1)S(1)} %get-tuple-element.32), channel_id=1, source_target_pairs={{0,4},{1,7},{2,6},{3,5},{4,0},{5,3},{6,2},{7,1},{8,12},{9,15},{10,... | collective-permute-start | bytes 196616 | tf_op jit(solution)/shard_map/ppermute | solution.py:307
  45.4 4.3 %collective-permute-start.10 = (bf16[4,4096]{1,0:T(4,128)(2,1)S(1)}, bf16[4,4096]{1,0:T(4,128)(2,1)S(1)}, u32[]{:S(2)}, u32[]{:S(2)}) collective-permute-start(bf16[4,4096]{1,0:T(4,128)(2,1)S(1)} %get-tuple-element.29), channel_id=1, source_target_pairs={{0,2},{1,3},{2,0},{3,1},{4,6},{5,7},{6,4},{7,5},{8,10},{9,11},{10,... | collective-permute-start | bytes 98312 | tf_op jit(solution)/shard_map/ppermute | solution.py:308
  50.4 1.3 %collective-permute-start.14 = (f32[4,4096]{1,0:T(4,128)S(1)}, f32[4,4096]{1,0:T(4,128)S(1)}, u32[]{:S(2)}, u32[]{:S(2)}) collective-permute-start(f32[4,4096]{1,0:T(4,128)S(1)} %get-tuple-element.34), channel_id=1, source_target_pairs={{0,1},{1,0},{2,3},{3,2},{4,5},{5,4},{6,7},{7,6},{8,9},{9,8},{10,11... | collective-permute-start | bytes 196616 | tf_op jit(solution)/shard_map/ppermute | solution.py:320

commit v3 on v2

--- a/solution.py
+++ b/solution.py
@@ -12,7 +12,7 @@
 ROW_TILE = 128
 VMEM_BYTES = 64 * 2**20
 EARLY_CHUNKS = 5
-RING_CHUNKS = 10
+RING_CHUNKS = 8
 NT = (((1,), (1,)), ((), ()))
 LINKED = ("expert", "rep")
 VMEM = pl.BlockSpec(memory_space=pltpu.VMEM)
@@ -245,9 +245,9 @@
         out_specs=VMEM,
         scratch_shapes=[pltpu.VMEM(array.shape, array.dtype) for array in (tokens, expert_ids, route_probs)]
         + [pltpu.SemaphoreType.DMA((3,))],
-        compiler_params=pltpu.CompilerParams(vmem_limit_bytes=VMEM_BYTES - 2**16),
+        compiler_params=pltpu.CompilerParams(vmem_limit_bytes=2**22),
         name="rows",
-    )(tokens, expert_ids, route_probs)
+    )(*[pltpu.with_memory_space_constraint(array, pltpu.HBM) for array in (tokens, expert_ids, route_probs)])
     shared_rows = lax.ppermute(mine, LINKED, chip_perm(chips, shared, shared))
     both = jnp.concatenate([mine, lax.ppermute(mine, LINKED, swap)], axis=0)
     fetched = [lax.ppermute(both, LINKED, chip_perm(chips, *pair)) for pair in pairs]

time: 52.6 us -> 50.9 us (0.968)
  other arithmetic: 0.8 us -> 0.04 us
  Pallas kernels: 27.4 us -> 26.8 us
    concatenate x1, other arithmetic: 0.8 us -> 0.04 us  [local(): both = jnp.concatenate([mine, lax.ppermute(mine, LINKED, swap)], axis=0)]
    pallas_call x1, Pallas kernels: 1.63 us -> 1.01 us  [local(): pl.pallas_call(functools.partial(rows_kernel, experts), out_shape=jax.Sha...]
where the time goes in v3:
time: 50.9 us; the launch traced here: 50.7 us
  Pallas kernels  26.8 us (53%)
  starting transfers between devices  15 us (29%)
  waiting for transfers between devices  8.83 us (17%)
    pallas_call x1, Pallas kernels, local(): pl.pallas_call(functools.partial(expert_kernel, len(pieces), per_block, e...  19.4 us
    ppermute x3, starting transfers between devices, local(): lax.ppermute(both, LINKED, chip_perm(chips, *pair))  6.72 us
    pallas_call x1, Pallas kernels, local(): pl.pallas_call(functools.partial(early_kernel, per_block), out_shape=(plt...  5.59 us
    ppermute x3, starting transfers between devices, local(): lax.ppermute(rows, LINKED, chip_perm(chips, *pair))  5.39 us
    ppermute x1, waiting for transfers between devices, local(): lax.ppermute(summed[-1], LINKED, chip_perm(chips, shared, shared))  3.73 us
    ppermute x1, waiting for transfers between devices, local(): lax.ppermute(other_part, LINKED, swap)  1.24 us
    ppermute x1, waiting for transfers between devices, local(): lax.ppermute(sent, LINKED, swap)  1.18 us
  transfers between devices with their start and end apart: 15, of which 8 were waited for; matrix products, arithmetic and copies ran while one was open for 0% of the time, Pallas kernels for 11%

profile of v3, /device:TPU:0, one launch (start us, length us, event | category | flops | bytes accessed | tf_op | source)
XLA Modules:
  0.0 50.7 jit_solution(11268842311406512907)
XLA Ops:
  0.0 1.0 %rows.1 = bf16[4,4224]{1,0:T(4,128)(2,1)S(1)} custom-call(bf16[4,4096]{1,0:T(4,128)(2,1)} %tokens_in.1, s32[4,8]{1,0:T(4,128)} %ids_in.1, f32[4,8]{1,0:T(4,128)} %probs_in.1), custom_call_target="tpu_custom_call" | custom-call | tf_op jit(solution)/shard_map/rows/pallas_call | solution.py:241
  1.0 0.5 %collective-permute-start = (bf16[4,4224]{1,0:T(4,128)(2,1)S(1)}, bf16[4,4224]{1,0:T(4,128)(2,1)S(1)}, u32[]{:S(2)}, u32[]{:S(2)}) collective-permute-start(bf16[4,4224]{1,0:T(4,128)(2,1)S(1)} %rows.1), channel_id=1, source_target_pairs={{0,1},{1,0},{2,3},{3,2},{4,5},{5,4},{6,7},{7,6},{8,9},{9,8},{10,11... | collective-permute-start | bytes 101384 | tf_op jit(solution)/shard_map/ppermute | solution.py:252
  1.5 0.9 %collective-permute-done = bf16[4,4224]{1,0:T(4,128)(2,1)S(1)} collective-permute-done((bf16[4,4224]{1,0:T(4,128)(2,1)S(1)}, bf16[4,4224]{1,0:T(4,128)(2,1)S(1)}, u32[]{:S(2)}, u32[]{:S(2)}) %collective-permute-start) | collective-permute-done | bytes 33824 | tf_op jit(solution)/shard_map/ppermute | solution.py:252
  2.4 3.0 %collective-permute-start.3 = (bf16[8,4224]{1,0:T(8,128)(2,1)S(1)}, bf16[8,4224]{1,0:T(8,128)(2,1)S(1)}, u32[]{:S(2)}, u32[]{:S(2)}) collective-permute-start(bf16[8,4224]{1,0:T(8,128)(2,1)S(1)} %pad_maximum_fusion.after_ref.refs_0_), channel_id=1, source_target_pairs={{0,4},{1,7},{2,6},{3,5},{4,0},{5,3},{6,2},{7,1},{8,12},{9,15},{10,... | collective-permute-start | bytes 202760 | tf_op jit(solution)/shard_map/ppermute | solution.py:253
  5.4 2.6 %collective-permute-start.2 = (bf16[8,4224]{1,0:T(8,128)(2,1)S(1)}, bf16[8,4224]{1,0:T(8,128)(2,1)S(1)}, u32[]{:S(2)}, u32[]{:S(2)}) collective-permute-start(bf16[8,4224]{1,0:T(8,128)(2,1)S(1)} %pad_maximum_fusion.after_ref.refs_0_), channel_id=1, source_target_pairs={{0,8},{1,11},{2,10},{3,9},{4,12},{5,15},{6,14},{7,13},{8,0},{9,3},... | collective-permute-start | bytes 202760 | tf_op jit(solution)/shard_map/ppermute | solution.py:253
  8.0 1.1 %collective-permute-start.1 = (bf16[8,4224]{1,0:T(8,128)(2,1)S(1)}, bf16[8,4224]{1,0:T(8,128)(2,1)S(1)}, u32[]{:S(2)}, u32[]{:S(2)}) collective-permute-start(bf16[8,4224]{1,0:T(8,128)(2,1)S(1)} %pad_maximum_fusion.after_ref.refs_0_), channel_id=1, source_target_pairs={{0,14},{1,13},{2,12},{3,15},{4,10},{5,9},{6,8},{7,11},{8,6},{9,5},... | collective-permute-start | bytes 202760 | tf_op jit(solution)/shard_map/ppermute | solution.py:253
  9.2 0.3 collective-permute-start.7
  9.5 5.6 %early_weights.1 = (bf16[5,384,4096]{2,1,0:T(8,128)(2,1)S(1)}, f32[8,128]{1,0:T(8,128)S(1)}) custom-call(bf16[8,4224]{1,0:T(8,128)(2,1)S(1)} %pad_maximum_fusion.after_ref.refs_0_, bf16[8,384,4096]{2,1,0:T(8,128)(2,1)} %refs_11_.1, bf16[8,384,4096]{2,1,0:T(8,128)(2,1)} %refs_12_.1, bf16[8,384,4096]{2,1,0:T(8,128)(2,1)} %refs_13_.1), custom_call_target="tpu_custom_call" | custom-call | bytes 31457280 | tf_op jit(solution)/shard_map/early_weights/pallas_call | solution.py:257
  15.1 0.0 collective-permute-done.3.refs_3_
  15.1 0.0 collective-permute-done.2.refs_2_
  15.1 0.3 collective-permute-done.1.refs_1_
  15.4 0.0 collective-permute-start.4
  15.4 0.5 collective-permute-start.5
  15.9 0.0 collective-permute-start.6
  15.9 0.0 collective-permute-done.7.refs_7_
  15.9 0.5 collective-permute-start.8
  16.4 0.9 %collective-permute-done.8.refs_8_ = bf16[4,4224]{1,0:T(4,128)(2,1)S(1)} collective-permute-done((bf16[4,4224]{1,0:T(4,128)(2,1)S(1)}, bf16[4,4224]{1,0:T(4,128)(2,1)S(1)}, u32[]{:S(2)}, u32[]{:S(2)}) %collective-permute-start.8) | collective-permute-done | bytes 33824 | tf_op jit(solution)/shard_map/ppermute | solution.py:272
  17.3 0.0 collective-permute-done.4.refs_4_
  17.3 0.0 collective-permute-done.5.refs_5_
  17.3 0.0 collective-permute-done.6.refs_6_
  17.3 19.4 %experts.1 = (f32[8,4096]{1,0:T(8,128)S(1)}, f32[32,4096]{1,0:T(8,128)S(1)}, bf16[32,4096]{1,0:T(8,128)(2,1)S(1)}) custom-call(bf16[8,4224]{1,0:T(8,128)(2,1)S(1)} %pad_maximum_fusion.after_ref.refs_0_, bf16[8,4224]{1,0:T(8,128)(2,1)S(1)} %collective-permute-done.1.refs_1_, bf16[8,4224]{1,0:T(8,128)(2,1)S(1)} %collective-permute-done.2.refs_2_, ...), custom_call_target="tpu_custom_call" | custom-call | flops 4831838208 | bytes 75497472 | tf_op jit(solution)/shard_map/experts/pallas_call | solution.py:275
  36.7 0.4 collective-permute-start.9
  37.2 1.2 %collective-permute-done.9.arrived_ref = bf16[32,4096]{1,0:T(8,128)(2,1)S(1)} collective-permute-done((bf16[32,4096]{1,0:T(8,128)(2,1)S(1)}, bf16[32,4096]{1,0:T(8,128)(2,1)S(1)}, u32[]{:S(2)}, u32[]{:S(2)}) %collective-permute-start.9) | collective-permute-done | bytes 262176 | tf_op jit(solution)/shard_map/ppermute | solution.py:304
  38.3 0.1 chip_sum.1
  38.4 4.6 %collective-permute-start.11 = (bf16[8,4096]{1,0:T(8,128)(2,1)S(1)}, bf16[8,4096]{1,0:T(8,128)(2,1)S(1)}, u32[]{:S(2)}, u32[]{:S(2)}) collective-permute-start(bf16[8,4096]{1,0:T(8,128)(2,1)S(1)} %get-tuple-element.30), channel_id=1, source_target_pairs={{0,14},{1,13},{2,12},{3,15},{4,10},{5,9},{6,8},{7,11},{8,6},{9,5},... | collective-permute-start | bytes 196616 | tf_op jit(solution)/shard_map/ppermute | solution.py:307
  43.0 0.0 collective-permute-start.12
  43.0 0.8 %collective-permute-start.13 = (bf16[8,4096]{1,0:T(8,128)(2,1)S(1)}, bf16[8,4096]{1,0:T(8,128)(2,1)S(1)}, u32[]{:S(2)}, u32[]{:S(2)}) collective-permute-start(bf16[8,4096]{1,0:T(8,128)(2,1)S(1)} %get-tuple-element.32), channel_id=1, source_target_pairs={{0,4},{1,7},{2,6},{3,5},{4,0},{5,3},{6,2},{7,1},{8,12},{9,15},{10,... | collective-permute-start | bytes 196616 | tf_op jit(solution)/shard_map/ppermute | solution.py:307
  43.8 0.5 %collective-permute-start.10 = (bf16[4,4096]{1,0:T(4,128)(2,1)S(1)}, bf16[4,4096]{1,0:T(4,128)(2,1)S(1)}, u32[]{:S(2)}, u32[]{:S(2)}) collective-permute-start(bf16[4,4096]{1,0:T(4,128)(2,1)S(1)} %get-tuple-element.29), channel_id=1, source_target_pairs={{0,2},{1,3},{2,0},{3,1},{4,6},{5,7},{6,4},{7,5},{8,10},{9,11},{10,... | collective-permute-start | bytes 98312 | tf_op jit(solution)/shard_map/ppermute | solution.py:308
  44.3 3.7 %collective-permute-done.10.shared_ref = bf16[4,4096]{1,0:T(4,128)(2,1)S(1)} collective-permute-done((bf16[4,4096]{1,0:T(4,128)(2,1)S(1)}, bf16[4,4096]{1,0:T(4,128)(2,1)S(1)}, u32[]{:S(2)}, u32[]{:S(2)}) %collective-permute-start.10) | collective-permute-done | bytes 32800 | tf_op jit(solution)/shard_map/ppermute | solution.py:308
  48.1 0.0 collective-permute-done.11.refs_0_
  48.1 0.2 collective-permute-done.12.refs_1_
  48.3 0.5 collective-permute-done.13.refs_2_
  48.8 0.1 collective-permute-start.14
  48.9 1.2 %collective-permute-done.14.other_ref = f32[4,4096]{1,0:T(4,128)S(1)} collective-permute-done((f32[4,4096]{1,0:T(4,128)S(1)}, f32[4,4096]{1,0:T(4,128)S(1)}, u32[]{:S(2)}, u32[]{:S(2)}) %collective-permute-start.14) | collective-permute-done | bytes 65568 | tf_op jit(solution)/shard_map/ppermute | solution.py:320
  50.1 0.6 %last_sum.1 = bf16[4,4096]{1,0:T(4,128)(2,1)} custom-call(f32[4,4096]{1,0:T(4,128)S(1)} %get-tuple-element.33.mine_ref, f32[4,4096]{1,0:T(4,128)S(1)} %collective-permute-done.14.other_ref), custom_call_target="tpu_custom_call" | custom-call | tf_op jit(solution)/shard_map/last_sum/pallas_call | solution.py:215
  (2 shorter events, 0.1 us)
Async XLA Ops:
  1.0 1.4 %collective-permute-start = (bf16[4,4224]{1,0:T(4,128)(2,1)S(1)}, bf16[4,4224]{1,0:T(4,128)(2,1)S(1)}, u32[]{:S(2)}, u32[]{:S(2)}) collective-permute-start(bf16[4,4224]{1,0:T(4,128)(2,1)S(1)} %rows.1), channel_id=1, source_target_pairs={{0,1},{1,0},{2,3},{3,2},{4,5},{5,4},{6,7},{7,6},{8,9},{9,8},{10,11... | collective-permute-start | bytes 101384 | tf_op jit(solution)/shard_map/ppermute | solution.py:252
  2.4 12.7 %collective-permute-start.3 = (bf16[8,4224]{1,0:T(8,128)(2,1)S(1)}, bf16[8,4224]{1,0:T(8,128)(2,1)S(1)}, u32[]{:S(2)}, u32[]{:S(2)}) collective-permute-start(bf16[8,4224]{1,0:T(8,128)(2,1)S(1)} %pad_maximum_fusion.after_ref.refs_0_), channel_id=1, source_target_pairs={{0,4},{1,7},{2,6},{3,5},{4,0},{5,3},{6,2},{7,1},{8,12},{9,15},{10,... | collective-permute-start | bytes 202760 | tf_op jit(solution)/shard_map/ppermute | solution.py:253
  5.4 9.7 %collective-permute-start.2 = (bf16[8,4224]{1,0:T(8,128)(2,1)S(1)}, bf16[8,4224]{1,0:T(8,128)(2,1)S(1)}, u32[]{:S(2)}, u32[]{:S(2)}) collective-permute-start(bf16[8,4224]{1,0:T(8,128)(2,1)S(1)} %pad_maximum_fusion.after_ref.refs_0_), channel_id=1, source_target_pairs={{0,8},{1,11},{2,10},{3,9},{4,12},{5,15},{6,14},{7,13},{8,0},{9,3},... | collective-permute-start | bytes 202760 | tf_op jit(solution)/shard_map/ppermute | solution.py:253
  8.0 7.4 %collective-permute-start.1 = (bf16[8,4224]{1,0:T(8,128)(2,1)S(1)}, bf16[8,4224]{1,0:T(8,128)(2,1)S(1)}, u32[]{:S(2)}, u32[]{:S(2)}) collective-permute-start(bf16[8,4224]{1,0:T(8,128)(2,1)S(1)} %pad_maximum_fusion.after_ref.refs_0_), channel_id=1, source_target_pairs={{0,14},{1,13},{2,12},{3,15},{4,10},{5,9},{6,8},{7,11},{8,6},{9,5},... | collective-permute-start | bytes 202760 | tf_op jit(solution)/shard_map/ppermute | solution.py:253
  9.2 6.8 %collective-permute-start.7 = (bf16[4,4224]{1,0:T(4,128)(2,1)S(1)}, bf16[4,4224]{1,0:T(4,128)(2,1)S(1)}, u32[]{:S(2)}, u32[]{:S(2)}) collective-permute-start(bf16[4,4224]{1,0:T(4,128)(2,1)S(1)} %rows.1), channel_id=1, source_target_pairs={{0,2},{1,3},{2,0},{3,1},{4,6},{5,7},{6,4},{7,5},{8,10},{9,11},{10,... | collective-permute-start | bytes 101384 | tf_op jit(solution)/shard_map/ppermute | solution.py:251
  15.4 1.9 %collective-permute-start.4 = (bf16[8,4224]{1,0:T(8,128)(2,1)S(1)}, bf16[8,4224]{1,0:T(8,128)(2,1)S(1)}, u32[]{:S(2)}, u32[]{:S(2)}) collective-permute-start(bf16[8,4224]{1,0:T(8,128)(2,1)S(1)} %collective-permute-done.1.refs_1_), channel_id=1, source_target_pairs={{0,1},{1,0},{2,3},{3,2},{4,5},{5,4},{6,7},{7,6},{8,9},{9,8},{10,11... | collective-permute-start | bytes 202760 | tf_op jit(solution)/shard_map/ppermute | solution.py:271
  15.4 1.9 %collective-permute-start.5 = (bf16[8,4224]{1,0:T(8,128)(2,1)S(1)}, bf16[8,4224]{1,0:T(8,128)(2,1)S(1)}, u32[]{:S(2)}, u32[]{:S(2)}) collective-permute-start(bf16[8,4224]{1,0:T(8,128)(2,1)S(1)} %collective-permute-done.2.refs_2_), channel_id=1, source_target_pairs={{0,1},{1,0},{2,3},{3,2},{4,5},{5,4},{6,7},{7,6},{8,9},{9,8},{10,11... | collective-permute-start | bytes 202760 | tf_op jit(solution)/shard_map/ppermute | solution.py:271
  15.9 1.4 %collective-permute-start.6 = (bf16[8,4224]{1,0:T(8,128)(2,1)S(1)}, bf16[8,4224]{1,0:T(8,128)(2,1)S(1)}, u32[]{:S(2)}, u32[]{:S(2)}) collective-permute-start(bf16[8,4224]{1,0:T(8,128)(2,1)S(1)} %collective-permute-done.3.refs_3_), channel_id=1, source_target_pairs={{0,1},{1,0},{2,3},{3,2},{4,5},{5,4},{6,7},{7,6},{8,9},{9,8},{10,11... | collective-permute-start | bytes 202760 | tf_op jit(solution)/shard_map/ppermute | solution.py:271
  15.9 1.3 %collective-permute-start.8 = (bf16[4,4224]{1,0:T(4,128)(2,1)S(1)}, bf16[4,4224]{1,0:T(4,128)(2,1)S(1)}, u32[]{:S(2)}, u32[]{:S(2)}) collective-permute-start(bf16[4,4224]{1,0:T(4,128)(2,1)S(1)} %collective-permute-done.7.refs_7_), channel_id=1, source_target_pairs={{0,1},{1,0},{2,3},{3,2},{4,5},{5,4},{6,7},{7,6},{8,9},{9,8},{10,11... | collective-permute-start | bytes 101384 | tf_op jit(solution)/shard_map/ppermute | solution.py:272
  36.7 1.6 %collective-permute-start.9 = (bf16[32,4096]{1,0:T(8,128)(2,1)S(1)}, bf16[32,4096]{1,0:T(8,128)(2,1)S(1)}, u32[]{:S(2)}, u32[]{:S(2)}) collective-permute-start(bf16[32,4096]{1,0:T(8,128)(2,1)S(1)} %get-tuple-element.28), channel_id=1, source_target_pairs={{0,1},{1,0},{2,3},{3,2},{4,5},{5,4},{6,7},{7,6},{8,9},{9,8},{10,11... | collective-permute-start | bytes 786440 | tf_op jit(solution)/shard_map/ppermute | solution.py:304
  38.4 9.7 %collective-permute-start.11 = (bf16[8,4096]{1,0:T(8,128)(2,1)S(1)}, bf16[8,4096]{1,0:T(8,128)(2,1)S(1)}, u32[]{:S(2)}, u32[]{:S(2)}) collective-permute-start(bf16[8,4096]{1,0:T(8,128)(2,1)S(1)} %get-tuple-element.30), channel_id=1, source_target_pairs={{0,14},{1,13},{2,12},{3,15},{4,10},{5,9},{6,8},{7,11},{8,6},{9,5},... | collective-permute-start | bytes 196616 | tf_op jit(solution)/shard_map/ppermute | solution.py:307
  43.0 5.3 %collective-permute-start.12 = (bf16[8,4096]{1,0:T(8,128)(2,1)S(1)}, bf16[8,4096]{1,0:T(8,128)(2,1)S(1)}, u32[]{:S(2)}, u32[]{:S(2)}) collective-permute-start(bf16[8,4096]{1,0:T(8,128)(2,1)S(1)} %get-tuple-element.31), channel_id=1, source_target_pairs={{0,8},{1,11},{2,10},{3,9},{4,12},{5,15},{6,14},{7,13},{8,0},{9,3},... | collective-permute-start | bytes 196616 | tf_op jit(solution)/shard_map/ppermute | solution.py:307
  43.0 5.7 %collective-permute-start.13 = (bf16[8,4096]{1,0:T(8,128)(2,1)S(1)}, bf16[8,4096]{1,0:T(8,128)(2,1)S(1)}, u32[]{:S(2)}, u32[]{:S(2)}) collective-permute-start(bf16[8,4096]{1,0:T(8,128)(2,1)S(1)} %get-tuple-element.32), channel_id=1, source_target_pairs={{0,4},{1,7},{2,6},{3,5},{4,0},{5,3},{6,2},{7,1},{8,12},{9,15},{10,... | collective-permute-start | bytes 196616 | tf_op jit(solution)/shard_map/ppermute | solution.py:307
  43.8 4.3 %collective-permute-start.10 = (bf16[4,4096]{1,0:T(4,128)(2,1)S(1)}, bf16[4,4096]{1,0:T(4,128)(2,1)S(1)}, u32[]{:S(2)}, u32[]{:S(2)}) collective-permute-start(bf16[4,4096]{1,0:T(4,128)(2,1)S(1)} %get-tuple-element.29), channel_id=1, source_target_pairs={{0,2},{1,3},{2,0},{3,1},{4,6},{5,7},{6,4},{7,5},{8,10},{9,11},{10,... | collective-permute-start | bytes 98312 | tf_op jit(solution)/shard_map/ppermute | solution.py:308
  48.8 1.3 %collective-permute-start.14 = (f32[4,4096]{1,0:T(4,128)S(1)}, f32[4,4096]{1,0:T(4,128)S(1)}, u32[]{:S(2)}, u32[]{:S(2)}) collective-permute-start(f32[4,4096]{1,0:T(4,128)S(1)} %get-tuple-element.34), channel_id=1, source_target_pairs={{0,1},{1,0},{2,3},{3,2},{4,5},{5,4},{6,7},{7,6},{8,9},{9,8},{10,11... | collective-permute-start | bytes 196616 | tf_op jit(solution)/shard_map/ppermute | solution.py:320

commit v4 on v3

--- a/solution.py
+++ b/solution.py
@@ -43,17 +43,17 @@
     return -(-2 * experts // LANES) * LANES
 
 
-def rows_kernel(experts, tokens_in, ids_in, probs_in, rows_ref, tokens_ref, ids_ref, probs_ref, sem):
-    width = tokens_ref.shape[1]
+def rows_kernel(experts, tokens_in, ids_in, probs_in, rows_ref, ids_ref, probs_ref, sem):
+    width = tokens_in.shape[1]
     copies = [
         pltpu.make_async_copy(source, target, sem.at[index])
         for index, (source, target) in enumerate(
-            [(ids_in, ids_ref), (probs_in, probs_ref), (tokens_in, tokens_ref)]
+            [(ids_in, ids_ref), (probs_in, probs_ref), (tokens_in, rows_ref.at[:, pl.ds(0, width)])]
         )
     ]
     for copy in copies:
         copy.start()
-    for copy in copies:
+    for copy in copies[:2]:
         copy.wait()
     probs = probs_ref[...]
     weights = probs / jnp.sum(probs, axis=1, keepdims=True)
@@ -65,8 +65,8 @@
         chosen = ids_ref[:, column : column + 1] == expert
         dense = dense + jnp.where(chosen, weights[:, column : column + 1], 0.0)
     high = dense.astype(jnp.bfloat16).astype(jnp.float32)
-    rows_ref[:, :width] = tokens_ref[...]
     rows_ref[:, width:] = jnp.where(lane < experts, high, dense - high).astype(jnp.bfloat16)
+    copies[2].wait()
 
 
 def chunk_of(refs, local_experts, per_block, index):
@@ -196,18 +196,19 @@
     ).astype(jnp.bfloat16)
 
 
-def token_sum_kernel(own_ref, shared_ref, *refs):
+def token_sum_kernel(own_ref, *refs):
     piece_refs, mine_ref, other_ref = refs[:-2], refs[-2], refs[-1]
     total = own_ref[...]
     for ref in piece_refs:
         total = total + ref[...].astype(jnp.float32)
     half = mine_ref.shape[0]
-    mine_ref[...] = total[:half, :] + shared_ref[...].astype(jnp.float32)
+    mine_ref[...] = total[:half, :]
     other_ref[...] = total[half:, :]
 
 
-def last_kernel(mine_ref, other_ref, out_ref):
-    out_ref[...] = (mine_ref[...] + other_ref[...]).astype(jnp.bfloat16)
+def last_kernel(mine_ref, shared_ref, other_ref, out_ref):
+    total = mine_ref[...] + shared_ref[...].astype(jnp.float32)
+    out_ref[...] = (total + other_ref[...]).astype(jnp.bfloat16)
 
 
 def call(kernel, out_shapes, *args, name):
@@ -243,7 +244,7 @@
         out_shape=jax.ShapeDtypeStruct((own_rows, width + padded_lanes(experts)), jnp.bfloat16),
         in_specs=[pl.BlockSpec(memory_space=pl.ANY)] * 3,
         out_specs=VMEM,
-        scratch_shapes=[pltpu.VMEM(array.shape, array.dtype) for array in (tokens, expert_ids, route_probs)]
+        scratch_shapes=[pltpu.VMEM(array.shape, array.dtype) for array in (expert_ids, route_probs)]
         + [pltpu.SemaphoreType.DMA((3,))],
         compiler_params=pltpu.CompilerParams(vmem_limit_bytes=2**22),
         name="rows",
@@ -310,13 +311,14 @@
     own_part, other_part = call(
         token_sum_kernel,
         [half, half],
-        *[in_vmem(array) for array in [own, shared_back] + returned],
+        *[in_vmem(array) for array in [own] + returned],
         name="token_sum",
     )
     return call(
         last_kernel,
         jax.ShapeDtypeStruct((own_rows, width), jnp.bfloat16),
         own_part,
+        shared_back,
         lax.ppermute(other_part, LINKED, swap),
         name="last_sum",
     )

time: 50.9 us -> 53.5 us (1.051)
  waiting for transfers between devices: 8.83 us -> 11.4 us
    ppermute x3, waiting for transfers between devices: 0.68 us -> 4.93 us  [local(): lax.ppermute(rows, LINKED, chip_perm(chips, *pair))]
    ppermute x1, waiting for transfers between devices: 1.24 us -> 0.01 us  [local(): lax.ppermute(other_part, LINKED, swap)]
  transfers between devices with their start and end apart: 15 -> 15, of which waited for: 8 -> 8; matrix products, arithmetic and copies ran while one was open for 0% -> 0% of each run, Pallas kernels for 11% -> 10%
where the time goes in v4:
time: 53.5 us; the launch traced here: 53.4 us
  Pallas kernels  26.7 us (50%)
  starting transfers between devices  15.2 us (28%)
  waiting for transfers between devices  11.4 us (21%)
    pallas_call x1, Pallas kernels, local(): pl.pallas_call(functools.partial(expert_kernel, len(pieces), per_block, e...  19.5 us
    ppermute x3, starting transfers between devices, local(): lax.ppermute(both, LINKED, chip_perm(chips, *pair))  6.72 us
    pallas_call x1, Pallas kernels, local(): pl.pallas_call(functools.partial(early_kernel, per_block), out_shape=(plt...  5.59 us
    ppermute x3, starting transfers between devices, local(): lax.ppermute(rows, LINKED, chip_perm(chips, *pair))  5.38 us
    ppermute x3, waiting for transfers between devices, local(): lax.ppermute(rows, LINKED, chip_perm(chips, *pair))  4.93 us
    ppermute x1, waiting for transfers between devices, local(): lax.ppermute(summed[-1], LINKED, chip_perm(chips, shared, shared))  3.26 us
    ppermute x1, waiting for transfers between devices, local(): lax.ppermute(sent, LINKED, swap)  1.19 us
  transfers between devices with their start and end apart: 15, of which 8 were waited for; matrix products, arithmetic and copies ran while one was open for 0% of the time, Pallas kernels for 10%

profile of v4, /device:TPU:0, one launch (start us, length us, event | category | flops | bytes accessed | tf_op | source)
XLA Modules:
  0.0 53.4 jit_solution(12134998282770343196)
XLA Ops:
  0.0 0.9 %rows.1 = bf16[4,4224]{1,0:T(4,128)(2,1)S(1)} custom-call(bf16[4,4096]{1,0:T(4,128)(2,1)} %tokens_in.1, s32[4,8]{1,0:T(4,128)} %ids_in.1, f32[4,8]{1,0:T(4,128)} %probs_in.1), custom_call_target="tpu_custom_call" | custom-call | tf_op jit(solution)/shard_map/rows/pallas_call | solution.py:242
  0.9 0.5 collective-permute-start
  1.4 0.9 %collective-permute-done = bf16[4,4224]{1,0:T(4,128)(2,1)S(1)} collective-permute-done((bf16[4,4224]{1,0:T(4,128)(2,1)S(1)}, bf16[4,4224]{1,0:T(4,128)(2,1)S(1)}, u32[]{:S(2)}, u32[]{:S(2)}) %collective-permute-start) | collective-permute-done | bytes 33824 | tf_op jit(solution)/shard_map/ppermute | solution.py:253
  2.3 3.0 %collective-permute-start.3 = (bf16[8,4224]{1,0:T(8,128)(2,1)S(1)}, bf16[8,4224]{1,0:T(8,128)(2,1)S(1)}, u32[]{:S(2)}, u32[]{:S(2)}) collective-permute-start(bf16[8,4224]{1,0:T(8,128)(2,1)S(1)} %pad_maximum_fusion.after_ref.refs_0_), channel_id=1, source_target_pairs={{0,4},{1,7},{2,6},{3,5},{4,0},{5,3},{6,2},{7,1},{8,12},{9,15},{10,... | collective-permute-start | bytes 202760 | tf_op jit(solution)/shard_map/ppermute | solution.py:254
  5.3 2.6 %collective-permute-start.2 = (bf16[8,4224]{1,0:T(8,128)(2,1)S(1)}, bf16[8,4224]{1,0:T(8,128)(2,1)S(1)}, u32[]{:S(2)}, u32[]{:S(2)}) collective-permute-start(bf16[8,4224]{1,0:T(8,128)(2,1)S(1)} %pad_maximum_fusion.after_ref.refs_0_), channel_id=1, source_target_pairs={{0,8},{1,11},{2,10},{3,9},{4,12},{5,15},{6,14},{7,13},{8,0},{9,3},... | collective-permute-start | bytes 202760 | tf_op jit(solution)/shard_map/ppermute | solution.py:254
  7.9 1.1 %collective-permute-start.1 = (bf16[8,4224]{1,0:T(8,128)(2,1)S(1)}, bf16[8,4224]{1,0:T(8,128)(2,1)S(1)}, u32[]{:S(2)}, u32[]{:S(2)}) collective-permute-start(bf16[8,4224]{1,0:T(8,128)(2,1)S(1)} %pad_maximum_fusion.after_ref.refs_0_), channel_id=1, source_target_pairs={{0,14},{1,13},{2,12},{3,15},{4,10},{5,9},{6,8},{7,11},{8,6},{9,5},... | collective-permute-start | bytes 202760 | tf_op jit(solution)/shard_map/ppermute | solution.py:254
  9.1 0.3 collective-permute-start.7
  9.4 5.6 %early_weights.1 = (bf16[5,384,4096]{2,1,0:T(8,128)(2,1)S(1)}, f32[8,128]{1,0:T(8,128)S(1)}) custom-call(bf16[8,4224]{1,0:T(8,128)(2,1)S(1)} %pad_maximum_fusion.after_ref.refs_0_, bf16[8,384,4096]{2,1,0:T(8,128)(2,1)} %refs_11_.1, bf16[8,384,4096]{2,1,0:T(8,128)(2,1)} %refs_12_.1, bf16[8,384,4096]{2,1,0:T(8,128)(2,1)} %refs_13_.1), custom_call_target="tpu_custom_call" | custom-call | bytes 31457280 | tf_op jit(solution)/shard_map/early_weights/pallas_call | solution.py:258
  15.0 0.0 collective-permute-done.3.refs_3_
  15.0 0.0 collective-permute-done.2.refs_2_
  15.0 0.3 collective-permute-done.1.refs_1_
  15.3 0.0 collective-permute-start.4
  15.3 0.5 collective-permute-start.5
  15.8 0.0 collective-permute-start.6
  15.8 0.0 collective-permute-done.7.refs_7_
  15.8 0.5 collective-permute-start.8
  16.3 0.9 %collective-permute-done.8.refs_8_ = bf16[4,4224]{1,0:T(4,128)(2,1)S(1)} collective-permute-done((bf16[4,4224]{1,0:T(4,128)(2,1)S(1)}, bf16[4,4224]{1,0:T(4,128)(2,1)S(1)}, u32[]{:S(2)}, u32[]{:S(2)}) %collective-permute-start.8) | collective-permute-done | bytes 33824 | tf_op jit(solution)/shard_map/ppermute | solution.py:273
  17.2 0.0 collective-permute-done.4.refs_4_
  17.2 0.0 collective-permute-done.5.refs_5_
  17.2 0.0 collective-permute-done.6.refs_6_
  17.2 19.5 %experts.1 = (f32[8,4096]{1,0:T(8,128)S(1)}, f32[32,4096]{1,0:T(8,128)S(1)}, bf16[32,4096]{1,0:T(8,128)(2,1)S(1)}) custom-call(bf16[8,4224]{1,0:T(8,128)(2,1)S(1)} %pad_maximum_fusion.after_ref.refs_0_, bf16[8,4224]{1,0:T(8,128)(2,1)S(1)} %collective-permute-done.1.refs_1_, bf16[8,4224]{1,0:T(8,128)(2,1)S(1)} %collective-permute-done.2.refs_2_, ...), custom_call_target="tpu_custom_call" | custom-call | flops 4831838208 | bytes 75497472 | tf_op jit(solution)/shard_map/experts/pallas_call | solution.py:276
  36.6 0.4 collective-permute-start.9
  37.1 1.2 %collective-permute-done.9.arrived_ref = bf16[32,4096]{1,0:T(8,128)(2,1)S(1)} collective-permute-done((bf16[32,4096]{1,0:T(8,128)(2,1)S(1)}, bf16[32,4096]{1,0:T(8,128)(2,1)S(1)}, u32[]{:S(2)}, u32[]{:S(2)}) %collective-permute-start.9) | collective-permute-done | bytes 262176 | tf_op jit(solution)/shard_map/ppermute | solution.py:305
  38.2 0.1 chip_sum.1
  38.3 4.6 %collective-permute-start.10 = (bf16[8,4096]{1,0:T(8,128)(2,1)S(1)}, bf16[8,4096]{1,0:T(8,128)(2,1)S(1)}, u32[]{:S(2)}, u32[]{:S(2)}) collective-permute-start(bf16[8,4096]{1,0:T(8,128)(2,1)S(1)} %get-tuple-element.29), channel_id=1, source_target_pairs={{0,14},{1,13},{2,12},{3,15},{4,10},{5,9},{6,8},{7,11},{8,6},{9,5},... | collective-permute-start | bytes 196616 | tf_op jit(solution)/shard_map/ppermute | solution.py:308
  42.9 0.0 collective-permute-start.11
  42.9 0.8 %collective-permute-start.12 = (bf16[8,4096]{1,0:T(8,128)(2,1)S(1)}, bf16[8,4096]{1,0:T(8,128)(2,1)S(1)}, u32[]{:S(2)}, u32[]{:S(2)}) collective-permute-start(bf16[8,4096]{1,0:T(8,128)(2,1)S(1)} %get-tuple-element.31), channel_id=1, source_target_pairs={{0,4},{1,7},{2,6},{3,5},{4,0},{5,3},{6,2},{7,1},{8,12},{9,15},{10,... | collective-permute-start | bytes 196616 | tf_op jit(solution)/shard_map/ppermute | solution.py:308
  43.7 2.0 %collective-permute-done.10.refs_0_ = bf16[8,4096]{1,0:T(8,128)(2,1)S(1)} collective-permute-done((bf16[8,4096]{1,0:T(8,128)(2,1)S(1)}, bf16[8,4096]{1,0:T(8,128)(2,1)S(1)}, u32[]{:S(2)}, u32[]{:S(2)}) %collective-permute-start.10) | collective-permute-done | bytes 65568 | tf_op jit(solution)/shard_map/ppermute | solution.py:308
  45.7 2.4 %collective-permute-done.11.refs_1_ = bf16[8,4096]{1,0:T(8,128)(2,1)S(1)} collective-permute-done((bf16[8,4096]{1,0:T(8,128)(2,1)S(1)}, bf16[8,4096]{1,0:T(8,128)(2,1)S(1)}, u32[]{:S(2)}, u32[]{:S(2)}) %collective-permute-start.11) | collective-permute-done | bytes 65568 | tf_op jit(solution)/shard_map/ppermute | solution.py:308
  48.2 0.5 collective-permute-done.12.refs_2_
  48.7 0.1 collective-permute-start.14
  48.8 0.7 %collective-permute-start.13 = (bf16[4,4096]{1,0:T(4,128)(2,1)S(1)}, bf16[4,4096]{1,0:T(4,128)(2,1)S(1)}, u32[]{:S(2)}, u32[]{:S(2)}) collective-permute-start(bf16[4,4096]{1,0:T(4,128)(2,1)S(1)} %get-tuple-element.33), channel_id=1, source_target_pairs={{0,2},{1,3},{2,0},{3,1},{4,6},{5,7},{6,4},{7,5},{8,10},{9,11},{10,... | collective-permute-start | bytes 98312 | tf_op jit(solution)/shard_map/ppermute | solution.py:309
  49.5 3.3 %collective-permute-done.13.shared_ref = bf16[4,4096]{1,0:T(4,128)(2,1)S(1)} collective-permute-done((bf16[4,4096]{1,0:T(4,128)(2,1)S(1)}, bf16[4,4096]{1,0:T(4,128)(2,1)S(1)}, u32[]{:S(2)}, u32[]{:S(2)}) %collective-permute-start.13) | collective-permute-done | bytes 32800 | tf_op jit(solution)/shard_map/ppermute | solution.py:309
  52.7 0.0 collective-permute-done.14.other_ref
  52.7 0.6 %last_sum.1 = bf16[4,4096]{1,0:T(4,128)(2,1)} custom-call(f32[4,4096]{1,0:T(4,128)S(1)} %get-tuple-element.32.mine_ref, bf16[4,4096]{1,0:T(4,128)(2,1)S(1)} %collective-permute-done.13.shared_ref, f32[4,4096]{1,0:T(4,128)S(1)} %collective-permute-done.14.other_ref), custom_call_target="tpu_custom_call" | custom-call | tf_op jit(solution)/shard_map/last_sum/pallas_call | solution.py:216
  (2 shorter events, 0.1 us)
Async XLA Ops:
  0.9 1.4 %collective-permute-start = (bf16[4,4224]{1,0:T(4,128)(2,1)S(1)}, bf16[4,4224]{1,0:T(4,128)(2,1)S(1)}, u32[]{:S(2)}, u32[]{:S(2)}) collective-permute-start(bf16[4,4224]{1,0:T(4,128)(2,1)S(1)} %rows.1), channel_id=1, source_target_pairs={{0,1},{1,0},{2,3},{3,2},{4,5},{5,4},{6,7},{7,6},{8,9},{9,8},{10,11... | collective-permute-start | bytes 101384 | tf_op jit(solution)/shard_map/ppermute | solution.py:253
  2.3 12.7 %collective-permute-start.3 = (bf16[8,4224]{1,0:T(8,128)(2,1)S(1)}, bf16[8,4224]{1,0:T(8,128)(2,1)S(1)}, u32[]{:S(2)}, u32[]{:S(2)}) collective-permute-start(bf16[8,4224]{1,0:T(8,128)(2,1)S(1)} %pad_maximum_fusion.after_ref.refs_0_), channel_id=1, source_target_pairs={{0,4},{1,7},{2,6},{3,5},{4,0},{5,3},{6,2},{7,1},{8,12},{9,15},{10,... | collective-permute-start | bytes 202760 | tf_op jit(solution)/shard_map/ppermute | solution.py:254
  5.3 9.7 %collective-permute-start.2 = (bf16[8,4224]{1,0:T(8,128)(2,1)S(1)}, bf16[8,4224]{1,0:T(8,128)(2,1)S(1)}, u32[]{:S(2)}, u32[]{:S(2)}) collective-permute-start(bf16[8,4224]{1,0:T(8,128)(2,1)S(1)} %pad_maximum_fusion.after_ref.refs_0_), channel_id=1, source_target_pairs={{0,8},{1,11},{2,10},{3,9},{4,12},{5,15},{6,14},{7,13},{8,0},{9,3},... | collective-permute-start | bytes 202760 | tf_op jit(solution)/shard_map/ppermute | solution.py:254
  7.9 7.4 %collective-permute-start.1 = (bf16[8,4224]{1,0:T(8,128)(2,1)S(1)}, bf16[8,4224]{1,0:T(8,128)(2,1)S(1)}, u32[]{:S(2)}, u32[]{:S(2)}) collective-permute-start(bf16[8,4224]{1,0:T(8,128)(2,1)S(1)} %pad_maximum_fusion.after_ref.refs_0_), channel_id=1, source_target_pairs={{0,14},{1,13},{2,12},{3,15},{4,10},{5,9},{6,8},{7,11},{8,6},{9,5},... | collective-permute-start | bytes 202760 | tf_op jit(solution)/shard_map/ppermute | solution.py:254
  9.1 6.8 %collective-permute-start.7 = (bf16[4,4224]{1,0:T(4,128)(2,1)S(1)}, bf16[4,4224]{1,0:T(4,128)(2,1)S(1)}, u32[]{:S(2)}, u32[]{:S(2)}) collective-permute-start(bf16[4,4224]{1,0:T(4,128)(2,1)S(1)} %rows.1), channel_id=1, source_target_pairs={{0,2},{1,3},{2,0},{3,1},{4,6},{5,7},{6,4},{7,5},{8,10},{9,11},{10,... | collective-permute-start | bytes 101384 | tf_op jit(solution)/shard_map/ppermute | solution.py:252
  15.3 1.9 %collective-permute-start.4 = (bf16[8,4224]{1,0:T(8,128)(2,1)S(1)}, bf16[8,4224]{1,0:T(8,128)(2,1)S(1)}, u32[]{:S(2)}, u32[]{:S(2)}) collective-permute-start(bf16[8,4224]{1,0:T(8,128)(2,1)S(1)} %collective-permute-done.1.refs_1_), channel_id=1, source_target_pairs={{0,1},{1,0},{2,3},{3,2},{4,5},{5,4},{6,7},{7,6},{8,9},{9,8},{10,11... | collective-permute-start | bytes 202760 | tf_op jit(solution)/shard_map/ppermute | solution.py:272
  15.3 1.9 %collective-permute-start.5 = (bf16[8,4224]{1,0:T(8,128)(2,1)S(1)}, bf16[8,4224]{1,0:T(8,128)(2,1)S(1)}, u32[]{:S(2)}, u32[]{:S(2)}) collective-permute-start(bf16[8,4224]{1,0:T(8,128)(2,1)S(1)} %collective-permute-done.2.refs_2_), channel_id=1, source_target_pairs={{0,1},{1,0},{2,3},{3,2},{4,5},{5,4},{6,7},{7,6},{8,9},{9,8},{10,11... | collective-permute-start | bytes 202760 | tf_op jit(solution)/shard_map/ppermute | solution.py:272
  15.8 1.4 %collective-permute-start.6 = (bf16[8,4224]{1,0:T(8,128)(2,1)S(1)}, bf16[8,4224]{1,0:T(8,128)(2,1)S(1)}, u32[]{:S(2)}, u32[]{:S(2)}) collective-permute-start(bf16[8,4224]{1,0:T(8,128)(2,1)S(1)} %collective-permute-done.3.refs_3_), channel_id=1, source_target_pairs={{0,1},{1,0},{2,3},{3,2},{4,5},{5,4},{6,7},{7,6},{8,9},{9,8},{10,11... | collective-permute-start | bytes 202760 | tf_op jit(solution)/shard_map/ppermute | solution.py:272
  15.8 1.3 %collective-permute-start.8 = (bf16[4,4224]{1,0:T(4,128)(2,1)S(1)}, bf16[4,4224]{1,0:T(4,128)(2,1)S(1)}, u32[]{:S(2)}, u32[]{:S(2)}) collective-permute-start(bf16[4,4224]{1,0:T(4,128)(2,1)S(1)} %collective-permute-done.7.refs_7_), channel_id=1, source_target_pairs={{0,1},{1,0},{2,3},{3,2},{4,5},{5,4},{6,7},{7,6},{8,9},{9,8},{10,11... | collective-permute-start | bytes 101384 | tf_op jit(solution)/shard_map/ppermute | solution.py:273
  36.6 1.6 %collective-permute-start.9 = (bf16[32,4096]{1,0:T(8,128)(2,1)S(1)}, bf16[32,4096]{1,0:T(8,128)(2,1)S(1)}, u32[]{:S(2)}, u32[]{:S(2)}) collective-permute-start(bf16[32,4096]{1,0:T(8,128)(2,1)S(1)} %get-tuple-element.28), channel_id=1, source_target_pairs={{0,1},{1,0},{2,3},{3,2},{4,5},{5,4},{6,7},{7,6},{8,9},{9,8},{10,11... | collective-permute-start | bytes 786440 | tf_op jit(solution)/shard_map/ppermute | solution.py:305
  38.3 7.4 %collective-permute-start.10 = (bf16[8,4096]{1,0:T(8,128)(2,1)S(1)}, bf16[8,4096]{1,0:T(8,128)(2,1)S(1)}, u32[]{:S(2)}, u32[]{:S(2)}) collective-permute-start(bf16[8,4096]{1,0:T(8,128)(2,1)S(1)} %get-tuple-element.29), channel_id=1, source_target_pairs={{0,14},{1,13},{2,12},{3,15},{4,10},{5,9},{6,8},{7,11},{8,6},{9,5},... | collective-permute-start | bytes 196616 | tf_op jit(solution)/shard_map/ppermute | solution.py:308
  42.9 5.3 %collective-permute-start.11 = (bf16[8,4096]{1,0:T(8,128)(2,1)S(1)}, bf16[8,4096]{1,0:T(8,128)(2,1)S(1)}, u32[]{:S(2)}, u32[]{:S(2)}) collective-permute-start(bf16[8,4096]{1,0:T(8,128)(2,1)S(1)} %get-tuple-element.30), channel_id=1, source_target_pairs={{0,8},{1,11},{2,10},{3,9},{4,12},{5,15},{6,14},{7,13},{8,0},{9,3},... | collective-permute-start | bytes 196616 | tf_op jit(solution)/shard_map/ppermute | solution.py:308
  42.9 5.7 %collective-permute-start.12 = (bf16[8,4096]{1,0:T(8,128)(2,1)S(1)}, bf16[8,4096]{1,0:T(8,128)(2,1)S(1)}, u32[]{:S(2)}, u32[]{:S(2)}) collective-permute-start(bf16[8,4096]{1,0:T(8,128)(2,1)S(1)} %get-tuple-element.31), channel_id=1, source_target_pairs={{0,4},{1,7},{2,6},{3,5},{4,0},{5,3},{6,2},{7,1},{8,12},{9,15},{10,... | collective-permute-start | bytes 196616 | tf_op jit(solution)/shard_map/ppermute | solution.py:308
  48.7 4.1 %collective-permute-start.14 = (f32[4,4096]{1,0:T(4,128)S(1)}, f32[4,4096]{1,0:T(4,128)S(1)}, u32[]{:S(2)}, u32[]{:S(2)}) collective-permute-start(f32[4,4096]{1,0:T(4,128)S(1)} %get-tuple-element.34), channel_id=1, source_target_pairs={{0,1},{1,0},{2,3},{3,2},{4,5},{5,4},{6,7},{7,6},{8,9},{9,8},{10,11... | collective-permute-start | bytes 196616 | tf_op jit(solution)/shard_map/ppermute | solution.py:322
  48.8 4.0 %collective-permute-start.13 = (bf16[4,4096]{1,0:T(4,128)(2,1)S(1)}, bf16[4,4096]{1,0:T(4,128)(2,1)S(1)}, u32[]{:S(2)}, u32[]{:S(2)}) collective-permute-start(bf16[4,4096]{1,0:T(4,128)(2,1)S(1)} %get-tuple-element.33), channel_id=1, source_target_pairs={{0,2},{1,3},{2,0},{3,1},{4,6},{5,7},{6,4},{7,5},{8,10},{9,11},{10,... | collective-permute-start | bytes 98312 | tf_op jit(solution)/shard_map/ppermute | solution.py:309
